TPU v7x, 32 devices: a whole 2x2x4 slice. The times are simulated.
32 devices in a mesh: dp: 8 (over z, x), tensor: 4 (over y, core).
Axes of the slice: x: 2, y: 2, z: 4, core: 2. Of those that a mesh axis runs over, the one named last changes fastest.
Arguments:
- layer_input: float32 [8, 1024, 768], P('dp', 'tensor'), may hold values from -40 to 40
- out_cotangent: float32 [8, 1024, 768], P('dp', 'tensor'), may hold values from -6 to 6
- mix_gain: bfloat16 [768], P('dp'), may hold values from 0.099609375 to 1.8984375
- mix_shift: bfloat16 [768], P('dp'), may hold values from -4 to 4
- query_weight: bfloat16 [768, 768], P('dp', 'tensor'), may hold values from -2 to 2
- query_bias: bfloat16 [64, 12], P('dp', 'tensor'), may hold values from -3 to 3
- key_weight: bfloat16 [768, 768], P('dp', 'tensor'), may hold values from -2 to 2
- value_weight: bfloat16 [768, 768], P('dp', 'tensor'), may hold values from -0.21875 to 0.21875
- value_bias: bfloat16 [64, 12], P('dp', 'tensor'), may hold values from -0.59765625 to 0.59765625
- output_weight: bfloat16 [768, 768], P('dp', 'tensor'), may hold values from -1.75 to 1.75
- output_bias: bfloat16 [768], P('dp'), may hold values from -4 to 4
- feed_gain: bfloat16 [768], P('dp'), may hold values from 0.099609375 to 1.8984375
- feed_shift: bfloat16 [768], P('dp'), may hold values from -4 to 4
- inner_weight: bfloat16 [768, 3072], P('dp', 'tensor'), may hold values from -0.21875 to 0.21875
- inner_bias: bfloat16 [64, 48], P('dp', 'tensor'), may hold values from -3 to 3
- outer_weight: bfloat16 [768, 3072], P('dp', 'tensor'), may hold values from -0.3125 to 0.3125
- outer_bias: bfloat16 [768], P('dp'), may hold values from -4 to 4
Outputs:
- layer_output: float32 [8, 1024, 768], P('dp', 'tensor')
- input_grad: float32 [8, 1024, 768], P('dp', 'tensor')
- mix_gain_grad: float32 [768], P(('dp', 'tensor'))
- mix_shift_grad: float32 [768], P(('dp', 'tensor'))
- query_weight_grad: float32 [768, 768], P('dp', 'tensor')
- query_bias_grad: float32 [64, 12], P('dp', 'tensor')
- key_weight_grad: float32 [768, 768], P('dp', 'tensor')
- value_weight_grad: float32 [768, 768], P('dp', 'tensor')
- value_bias_grad: float32 [64, 12], P('dp', 'tensor')
- output_weight_grad: float32 [768, 768], P('dp', 'tensor')
- output_bias_grad: float32 [768], P(('dp', 'tensor'))
- feed_gain_grad: float32 [768], P(('dp', 'tensor'))
- feed_shift_grad: float32 [768], P(('dp', 'tensor'))
- inner_weight_grad: float32 [768, 3072], P('dp', 'tensor')
- inner_bias_grad: float32 [64, 48], P('dp', 'tensor')
- outer_weight_grad: float32 [768, 3072], P('dp', 'tensor')
- outer_bias_grad: float32 [768], P(('dp', 'tensor'))
All inputs are finite; a program needn't handle non-finite values.
Results may differ from a plain program's by a relative error of at most 0.02.
Values may be sent and summed in bfloat16 or wider, within the bound.
A program may use at most 128 MiB of HBM per device.

v0:
```python
import math

import jax
import jax.numpy as jnp
from jax import lax
from jax.sharding import PartitionSpec as P

HD = 64


EPS = 1e-05
ROOT_HALF = 0.7071067811865476
DENSITY_NORM = 0.3989422804014327


def layer_norm(block, gain, shift):
    row_mean = jnp.mean(block, axis=-1, keepdims=True)
    centred = block - row_mean
    rstd = lax.rsqrt(jnp.mean(centred * centred, axis=-1, keepdims=True) + EPS)
    normed = centred * rstd
    lowered = (normed * gain.astype(jnp.float32) + shift.astype(jnp.float32)).astype(jnp.bfloat16)
    return (normed, rstd, lowered)


def norm_backward(gradient, normed, rstd, gain):
    scaled = gradient * gain.astype(jnp.float32)
    first = jnp.mean(scaled, axis=-1, keepdims=True)
    second = jnp.mean(scaled * normed, axis=-1, keepdims=True)
    return (scaled - first - normed * second) * rstd


def gelu_value(preact):
    return 0.5 * preact * (1.0 + lax.erf(preact * ROOT_HALF))


def gelu_slope(preact):
    return 0.5 * (1.0 + lax.erf(preact * ROOT_HALF)) + preact * DENSITY_NORM * jnp.exp(
        -0.5 * preact * preact
    )


def matmul(left, right):
    return jnp.dot(left, right, preferred_element_type=jnp.float32)


def token_product(left, right):
    return lax.dot_general(
        left, right, (((0,), (0,)), ((), ())), preferred_element_type=jnp.float32
    )


def split_heads(block):
    return block.reshape(block.shape[0], block.shape[1] // HD, HD)


def attend(operands):
    queries, key_rows, values = operands
    score_scale = 1.0 / math.sqrt(HD)
    scores = (
        jnp.einsum(
            "qhd,khd->hqk",
            split_heads(queries),
            split_heads(key_rows),
            preferred_element_type=jnp.float32,
        )
        * score_scale
    )
    row_max = jnp.max(scores, axis=-1, keepdims=True)
    log_total = row_max + jnp.log(jnp.sum(jnp.exp(scores - row_max), axis=-1, keepdims=True))
    prob_low = jnp.exp(scores - log_total).astype(jnp.bfloat16)
    context = jnp.einsum(
        "hqk,khd->qhd", prob_low, split_heads(values), preferred_element_type=jnp.float32
    )
    return (context.reshape(queries.shape).astype(jnp.bfloat16), log_total)


def attend_back(operands):
    queries, key_rows, values, context_grad, log_total = operands
    score_scale = 1.0 / math.sqrt(HD)
    query_heads = split_heads(queries)
    key_heads = split_heads(key_rows)
    grad_heads = split_heads(context_grad)
    scores = (
        jnp.einsum("qhd,khd->hqk", query_heads, key_heads, preferred_element_type=jnp.float32)
        * score_scale
    )
    prob_full = jnp.exp(scores - log_total)
    prob_low = prob_full.astype(jnp.bfloat16)
    value_grad = jnp.einsum(
        "hqk,qhd->khd", prob_low, grad_heads, preferred_element_type=jnp.float32
    )
    prob_grad = jnp.einsum(
        "qhd,khd->hqk", grad_heads, split_heads(values), preferred_element_type=jnp.float32
    )
    row_dot = jnp.sum(prob_full * prob_grad, axis=-1, keepdims=True)
    score_grad = (prob_full * (prob_grad - row_dot) * score_scale).astype(jnp.bfloat16)
    query_grad = jnp.einsum(
        "hqk,khd->qhd", score_grad, key_heads, preferred_element_type=jnp.float32
    )
    key_low = jnp.einsum(
        "hqk,qhd->khd", score_grad, query_heads, preferred_element_type=jnp.float32
    ).astype(jnp.bfloat16)
    return (
        query_grad.reshape(queries.shape),
        key_low.reshape(queries.shape),
        value_grad.reshape(queries.shape),
    )


def on_device(
    layer_input,
    out_cotangent,
    mix_gain,
    mix_shift,
    query_weight,
    query_bias,
    key_weight,
    value_weight,
    value_bias,
    output_weight,
    output_bias,
    feed_gain,
    feed_shift,
    inner_weight,
    inner_bias,
    outer_weight,
    outer_bias,
):
    (
        gain_first,
        shift_first,
        query_full,
        bias_query,
        key_full,
        value_full,
        bias_value,
        output_full,
        bias_output,
        gain_second,
        shift_second,
        inner_full,
        bias_inner,
        outer_full,
        bias_outer,
    ) = (
        lax.all_gather(mix_gain, "dp", axis=0, tiled=True),
        lax.all_gather(mix_shift, "dp", axis=0, tiled=True),
        lax.all_gather(query_weight, "dp", axis=0, tiled=True),
        lax.all_gather(query_bias, "dp", axis=0, tiled=True),
        lax.all_gather(key_weight, "dp", axis=0, tiled=True),
        lax.all_gather(value_weight, "dp", axis=0, tiled=True),
        lax.all_gather(value_bias, "dp", axis=0, tiled=True),
        lax.all_gather(output_weight, "dp", axis=0, tiled=True),
        lax.all_gather(output_bias, "dp", axis=0, tiled=True),
        lax.all_gather(feed_gain, "dp", axis=0, tiled=True),
        lax.all_gather(feed_shift, "dp", axis=0, tiled=True),
        lax.all_gather(inner_weight, "dp", axis=0, tiled=True),
        lax.all_gather(inner_bias, "dp", axis=0, tiled=True),
        lax.all_gather(outer_weight, "dp", axis=0, tiled=True),
        lax.all_gather(outer_bias, "dp", axis=0, tiled=True),
    )
    clip_count = layer_input.shape[0]
    feature_count = layer_input.shape[2]
    normed_one, rstd_one, lowered_one = layer_norm(layer_input, gain_first, shift_first)
    gathered_one = lax.all_gather(lowered_one, "tensor", axis=1, tiled=True)
    frames = gathered_one.shape[1]
    flat_one = gathered_one.reshape(clip_count * frames, feature_count)
    vector_query = bias_query.astype(jnp.float32).T.reshape(-1)
    vector_value = bias_value.astype(jnp.float32).T.reshape(-1)
    vector_inner = bias_inner.astype(jnp.float32).T.reshape(-1)
    width = query_full.shape[1]
    queries = (matmul(flat_one, query_full) + vector_query).astype(jnp.bfloat16)
    key_rows = matmul(flat_one, key_full).astype(jnp.bfloat16)
    values = (matmul(flat_one, value_full) + vector_value).astype(jnp.bfloat16)
    clip_queries = queries.reshape(clip_count, frames, width)
    clip_keys = key_rows.reshape(clip_count, frames, width)
    clip_values = values.reshape(clip_count, frames, width)
    context, log_total = lax.map(attend, (clip_queries, clip_keys, clip_values))
    flat_context = context.reshape(clip_count * frames, width)
    attn_partial = matmul(flat_context, output_full.T).reshape(clip_count, frames, feature_count)
    attn_share = lax.psum_scatter(
        attn_partial.astype(jnp.bfloat16), "tensor", scatter_dimension=1, tiled=True
    ).astype(jnp.float32)
    mixed = layer_input + attn_share + bias_output.astype(jnp.float32)
    normed_two, rstd_two, lowered_two = layer_norm(mixed, gain_second, shift_second)
    gathered_two = lax.all_gather(lowered_two, "tensor", axis=1, tiled=True)
    flat_two = gathered_two.reshape(clip_count * frames, feature_count)
    preact = matmul(flat_two, inner_full) + vector_inner
    hidden = gelu_value(preact).astype(jnp.bfloat16)
    feed_partial = matmul(hidden, outer_full.T).reshape(clip_count, frames, feature_count)
    feed_share = lax.psum_scatter(
        feed_partial.astype(jnp.bfloat16), "tensor", scatter_dimension=1, tiled=True
    ).astype(jnp.float32)
    layer_output = mixed + feed_share + bias_outer.astype(jnp.float32)
    cot_low = out_cotangent.astype(jnp.bfloat16)
    cot_all = lax.all_gather(cot_low, "tensor", axis=1, tiled=True).reshape(
        clip_count * frames, feature_count
    )
    preact_grad = matmul(cot_all, outer_full) * gelu_slope(preact)
    preact_low = preact_grad.astype(jnp.bfloat16)
    outer_grad = token_product(cot_all, hidden)
    inner_grad = token_product(flat_two, preact_low)
    inner_bias_part = jnp.sum(preact_grad, axis=0).reshape(-1, HD).T
    norm_two_part = matmul(preact_low, inner_full.T).reshape(clip_count, frames, feature_count)
    norm_two_grad = lax.psum_scatter(
        norm_two_part.astype(jnp.bfloat16), "tensor", scatter_dimension=1, tiled=True
    ).astype(jnp.float32)
    feed_gain_part = jnp.sum(norm_two_grad * normed_two, axis=(0, 1))
    feed_shift_part = jnp.sum(norm_two_grad, axis=(0, 1))
    mixed_grad = out_cotangent + norm_backward(norm_two_grad, normed_two, rstd_two, gain_second)
    outer_bias_part = jnp.sum(out_cotangent, axis=(0, 1))
    output_bias_part = jnp.sum(mixed_grad, axis=(0, 1))
    mixed_low = mixed_grad.astype(jnp.bfloat16)
    mixed_all = lax.all_gather(mixed_low, "tensor", axis=1, tiled=True).reshape(
        clip_count * frames, feature_count
    )
    output_grad = token_product(mixed_all, flat_context)
    context_grad = (
        matmul(mixed_all, output_full).astype(jnp.bfloat16).reshape(clip_count, frames, width)
    )
    query_grad, key_low, value_grad = lax.map(
        attend_back, (clip_queries, clip_keys, clip_values, context_grad, log_total)
    )
    query_grad = query_grad.reshape(clip_count * frames, width)
    key_low = key_low.reshape(clip_count * frames, width)
    value_grad = value_grad.reshape(clip_count * frames, width)
    query_low = query_grad.astype(jnp.bfloat16)
    value_low = value_grad.astype(jnp.bfloat16)
    query_grad_part = token_product(flat_one, query_low)
    key_grad_part = token_product(flat_one, key_low)
    value_grad_part = token_product(flat_one, value_low)
    query_bias_part = jnp.sum(query_grad, axis=0).reshape(-1, HD).T
    value_bias_part = jnp.sum(value_grad, axis=0).reshape(-1, HD).T
    norm_one_part = (
        matmul(query_low, query_full.T)
        + matmul(key_low, key_full.T)
        + matmul(value_low, value_full.T)
    )
    norm_one_grad = lax.psum_scatter(
        norm_one_part.reshape(clip_count, frames, feature_count).astype(jnp.bfloat16),
        "tensor",
        scatter_dimension=1,
        tiled=True,
    ).astype(jnp.float32)
    mix_gain_part = jnp.sum(norm_one_grad * normed_one, axis=(0, 1))
    mix_shift_part = jnp.sum(norm_one_grad, axis=(0, 1))
    input_grad = mixed_grad + norm_backward(norm_one_grad, normed_one, rstd_one, gain_first)
    (
        query_weight_grad,
        query_bias_grad,
        key_weight_grad,
        value_weight_grad,
        value_bias_grad,
        output_weight_grad,
        inner_weight_grad,
        inner_bias_grad,
        outer_weight_grad,
    ) = (
        lax.psum_scatter(query_grad_part, "dp", scatter_dimension=0, tiled=True),
        lax.psum_scatter(query_bias_part, "dp", scatter_dimension=0, tiled=True),
        lax.psum_scatter(key_grad_part, "dp", scatter_dimension=0, tiled=True),
        lax.psum_scatter(value_grad_part, "dp", scatter_dimension=0, tiled=True),
        lax.psum_scatter(value_bias_part, "dp", scatter_dimension=0, tiled=True),
        lax.psum_scatter(output_grad, "dp", scatter_dimension=0, tiled=True),
        lax.psum_scatter(inner_grad, "dp", scatter_dimension=0, tiled=True),
        lax.psum_scatter(inner_bias_part, "dp", scatter_dimension=0, tiled=True),
        lax.psum_scatter(outer_grad, "dp", scatter_dimension=0, tiled=True),
    )
    (
        mix_gain_grad,
        mix_shift_grad,
        output_bias_grad,
        feed_gain_grad,
        feed_shift_grad,
        outer_bias_grad,
    ) = (
        lax.psum_scatter(mix_gain_part, ("dp", "tensor"), scatter_dimension=0, tiled=True),
        lax.psum_scatter(mix_shift_part, ("dp", "tensor"), scatter_dimension=0, tiled=True),
        lax.psum_scatter(output_bias_part, ("dp", "tensor"), scatter_dimension=0, tiled=True),
        lax.psum_scatter(feed_gain_part, ("dp", "tensor"), scatter_dimension=0, tiled=True),
        lax.psum_scatter(feed_shift_part, ("dp", "tensor"), scatter_dimension=0, tiled=True),
        lax.psum_scatter(outer_bias_part, ("dp", "tensor"), scatter_dimension=0, tiled=True),
    )
    return (
        layer_output,
        input_grad,
        mix_gain_grad,
        mix_shift_grad,
        query_weight_grad,
        query_bias_grad,
        key_weight_grad,
        value_weight_grad,
        value_bias_grad,
        output_weight_grad,
        output_bias_grad,
        feed_gain_grad,
        feed_shift_grad,
        inner_weight_grad,
        inner_bias_grad,
        outer_weight_grad,
        outer_bias_grad,
    )


def solution(mesh):
    placed = (
        P("dp", "tensor", None),
        P("dp", "tensor", None),
        P("dp"),
        P("dp"),
        P("dp", "tensor"),
        P("dp", "tensor"),
        P("dp", "tensor"),
        P("dp", "tensor"),
        P("dp", "tensor"),
        P("dp", "tensor"),
        P("dp"),
        P("dp"),
        P("dp"),
        P("dp", "tensor"),
        P("dp", "tensor"),
        P("dp", "tensor"),
        P("dp"),
    )
    return jax.shard_map(
        on_device,
        mesh=mesh,
        in_specs=placed,
        out_specs=(
            P("dp", "tensor", None),
            P("dp", "tensor", None),
            P(("dp", "tensor")),
            P(("dp", "tensor")),
            P("dp", "tensor"),
            P("dp", "tensor"),
            P("dp", "tensor"),
            P("dp", "tensor"),
            P("dp", "tensor"),
            P("dp", "tensor"),
            P(("dp", "tensor")),
            P(("dp", "tensor")),
            P(("dp", "tensor")),
            P("dp", "tensor"),
            P("dp", "tensor"),
            P("dp", "tensor"),
            P(("dp", "tensor")),
        ),
        check_vma=False,
    )
```

profile of v0, /device:TPU:0, one launch (start us, length us, event | category | flops | bytes accessed | tf_op | source)
XLA Modules:
  0.0 956.4 jit_solution(9160846206304437627)
XLA Ops:
  17.8 38.8 %all-reduce.17 = (bf16[768]{0:T(1024)(128)(2,1)S(1)}, bf16[768]{0:T(1024)(128)(2,1)S(1)}, bf16[768]{0:T(1024)(128)(2,1)S(1)}, bf16[768]{0:T(1024)(128)(2,1)S(1)}...) all-reduce(bf16[768]{0:T(1024)(128)(2,1)S(1)} %dynamic-update-slice., ...), channel_id=1, replica_groups=mesh['dp'=8,'tensor'=4] {'dp'}, use_global_device_ids=true, to_apply=%add.1 | all-reduce | flops 4608 | bytes 18432
  58.8 16.6 %all-gather.1 = bf16[8,8,3]{1,2,0:T(4,128)(2,1)S(1)} all-gather(bf16[1,8,3]{1,2,0:T(4,128)(2,1)S(1)} %bitcast.145), channel_id=1, replica_groups=mesh['dp'=8,'tensor'=4] {'dp'}, dimensions={0}, use_global_device_ids=true | all-gather | bytes 432 | tf_op jit(solution)/shard_map/all_gather | solution.py:149
  75.6 17.9 %all-gather = bf16[8,8,3]{1,2,0:T(4,128)(2,1)S(1)} all-gather(bf16[1,8,3]{1,2,0:T(4,128)(2,1)S(1)} %bitcast.146), channel_id=1, replica_groups=mesh['dp'=8,'tensor'=4] {'dp'}, dimensions={0}, use_global_device_ids=true | all-gather | bytes 432 | tf_op jit(solution)/shard_map/all_gather | solution.py:152
  93.7 31.1 %all_gather.62 = bf16[768,192]{1,0:T(8,128)(2,1)S(1)} all-gather(bf16[96,192]{1,0:T(8,128)(2,1)S(1)} %copy-done.22), channel_id=1, replica_groups=mesh['dp'=8,'tensor'=4] {'dp'}, dimensions={0}, use_global_device_ids=true | all-gather | bytes 331776 | tf_op jit(solution)/shard_map/all_gather | solution.py:148
  124.8 31.1 %all_gather.64 = bf16[768,192]{1,0:T(8,128)(2,1)S(1)} all-gather(bf16[96,192]{1,0:T(8,128)(2,1)S(1)} %copy-done.23), channel_id=1, replica_groups=mesh['dp'=8,'tensor'=4] {'dp'}, dimensions={0}, use_global_device_ids=true | all-gather | bytes 331776 | tf_op jit(solution)/shard_map/all_gather | solution.py:150
  155.9 31.1 %all_gather.60 = bf16[768,192]{1,0:T(8,128)(2,1)S(1)} all-gather(bf16[96,192]{1,0:T(8,128)(2,1)S(1)} %copy-done.24), channel_id=1, replica_groups=mesh['dp'=8,'tensor'=4] {'dp'}, dimensions={0}, use_global_device_ids=true | all-gather | bytes 331776 | tf_op jit(solution)/shard_map/all_gather | solution.py:151
  187.0 31.0 %all_gather.65 = bf16[768,192]{1,0:T(8,128)(2,1)S(1)} all-gather(bf16[96,192]{1,0:T(8,128)(2,1)S(1)} %copy-done.25), channel_id=1, replica_groups=mesh['dp'=8,'tensor'=4] {'dp'}, dimensions={0}, use_global_device_ids=true | all-gather | bytes 331776 | tf_op jit(solution)/shard_map/all_gather | solution.py:153
  236.3 23.1 %reduce-scatter.16.cloned.1.call-done = bf16[1,256,768]{2,1,0:T(8,128)(2,1)} async-done(((bf16[1,1024,768]{2,1,0:T(8,128)(2,1)}), bf16[1,256,768]{2,1,0:T(8,128)(2,1)}) %reduce-scatter.16.cloned.1.call-update) | async-done | bytes 393232 | tf_op jit(solution)/shard_map/reduce_scatter | solution.py:181
  267.0 26.2 %all_gather.71 = bf16[64,12]{1,0:T(8,128)(2,1)S(1)} all-gather(bf16[8,12]{1,0:T(8,128)(2,1)} %param.31), channel_id=1, replica_groups=mesh['dp'=8,'tensor'=4] {'dp'}, dimensions={0}, use_global_device_ids=true | all-gather | bytes 1728 | tf_op jit(solution)/shard_map/all_gather | solution.py:158
  296.6 5.5 multiply_convert_fusion.1
  302.1 37.4 %all-gather.15.cloned.1.call-done = bf16[768,768]{1,0:T(8,128)(2,1)} async-done(((bf16[96,768]{1,0:T(8,128)(2,1)}), bf16[768,768]{1,0:T(8,128)(2,1)}) %all-gather.15.cloned.1.call-update) | async-done | bytes 1179664 | tf_op jit(solution)/shard_map/all_gather | solution.py:159
  339.5 20.3 %all-gather.17.cloned.1.call-done = bf16[1,1024,768]{2,1,0:T(8,128)(2,1)} async-done(((bf16[1,256,768]{2,1,0:T(8,128)(2,1)}), bf16[1,1024,768]{2,1,0:T(8,128)(2,1)}) %all-gather.17.cloned.1.call-update) | async-done | bytes 1572880 | tf_op jit(solution)/shard_map/all_gather | solution.py:196
  359.7 5.5 fusion.110
  369.0 4.4 fusion.46
  374.7 22.5 %reduce-scatter.20.cloned.1.call-done = bf16[1,256,768]{2,1,0:T(8,128)(2,1)} async-done(((bf16[1,1024,768]{2,1,0:T(8,128)(2,1)}), bf16[1,256,768]{2,1,0:T(8,128)(2,1)}) %reduce-scatter.20.cloned.1.call-update) | async-done | bytes 393232 | tf_op jit(solution)/shard_map/reduce_scatter | solution.py:205
  399.9 28.0 %reduce-scatter.18.cloned.1.call-done = bf16[1,256,768]{2,1,0:T(8,128)(2,1)} async-done(((bf16[1,1024,768]{2,1,0:T(8,128)(2,1)}), bf16[1,256,768]{2,1,0:T(8,128)(2,1)}) %reduce-scatter.18.cloned.1.call-update) | async-done | bytes 393232 | tf_op jit(solution)/shard_map/reduce_scatter | solution.py:191
  427.8 3.3 fusion.101
  432.9 19.6 %all-gather.19.cloned.1.call-done = bf16[1,1024,768]{2,1,0:T(8,128)(2,1)} async-done(((bf16[1,256,768]{2,1,0:T(8,128)(2,1)}), bf16[1,1024,768]{2,1,0:T(8,128)(2,1)}) %all-gather.19.cloned.1.call-update) | async-done | bytes 1572880 | tf_op jit(solution)/shard_map/all_gather | solution.py:214
  454.6 7.5 fusion.104
  462.1 6.3 fusion.111
  468.4 19.8 %fusion.70 = bf16[3,64,1024]{2,1,0:T(8,128)(2,1)} fusion(bf16[1024,3,64]{0,2,1:T(8,128)(2,1)S(1)} %bitcast.135, f32[3,1024,1024]{1,2,0:T(8,128)} %fusion.111, f32[3,1024,1024]{1,2,0:T(8,128)} %copy-done, f32[3,1024]{1,0:T(4,128)S(1)} %log_add_fusion), kind=kOutput, calls=%fused_computation.61 | convolution fusion | flops 431165440 | bytes 25964544 | tf_op jit(solution)/shard_map/while/body/eval_jaxpr/hqk,qhd->khd/dot_general | solution.py:100
  488.3 20.0 %fusion.105 = (f32[3,64]{1,0:T(4,128)}, bf16[1024,3,64]{0,2,1:T(8,128)(2,1)}) fusion(bf16[1024,3,64]{0,2,1:T(8,128)(2,1)S(1)} %bitcast.133, f32[3,1024,1024]{1,2,0:T(8,128)} %fusion.111, f32[3,1024,1024]{1,2,0:T(8,128)} %copy-done, f32[3,1024]{1,0:T(4,128)S(1)} %log_add_fusion), kind=kOutput, calls=%fused_computation.118 | convolution fusion | flops 431361856 | bytes 25965312 | tf_op jit(solution)/shard_map/while/body/eval_jaxpr/hqk,khd->qhd/dot_general | solution.py:97
  512.6 4.7 fusion.29
  517.4 4.8 convolution_bitcast_fusion
  522.3 3.1 copy.76
  535.0 37.5 %all-reduce.16 = (f32[64,3]{0,1:T(4,128)S(1)}, f32[64,3]{0,1:T(4,128)S(1)}, f32[64,12]{0,1:T(8,128)S(1)}) all-reduce(f32[64,3]{0,1:T(4,128)} %bitcast.144, f32[64,3]{0,1:T(4,128)} %bitcast.143, f32[64,12]{0,1:T(8,128)S(1)} %bitcast.140), channel_id=9, replica_groups=mesh['dp'=8,'tensor'=4] {'dp'}, use_global_device_ids=true, to_apply=%region_21.22.clone | all-reduce | flops 1152 | bytes 9216
  576.0 38.2 %all-reduce.15 = (f32[768]{0:T(1024)S(1)}, f32[768]{0:T(1024)S(1)}, f32[768]{0:T(1024)S(1)}, f32[768]{0:T(1024)S(1)}, f32[768]{0:T(1024)S(1)}, /*index=5*/f32[768]{0:T(1024)S(1)}) all-reduce(f32[768]{0:T(1024)S(1)} %get-tuple-element.132, f32[768]{0:T(1024)S(1)} %get-tuple-element.137, ...), channel_id=6, replica_groups=mesh['dp'=8,'tensor'=4] {'dp','tensor'}, use_global_device_ids=true, to_apply=%region_16.17.clone | all-reduce | flops 4608 | bytes 36864
  619.9 66.6 %reduce-scatter.34.cloned.1.call-done = f32[96,768]{1,0:T(8,128)} async-done(((f32[768,768]{1,0:T(8,128)}), f32[96,768]{1,0:T(8,128)}) %reduce-scatter.34.cloned.1.call-update) | async-done | bytes 294928
  686.5 65.5 %reduce-scatter.30.cloned.1.call-done = f32[96,192]{1,0:T(8,128)} async-done(((f32[768,192]{1,0:T(8,128)}), f32[96,192]{1,0:T(8,128)}) %reduce-scatter.30.cloned.1.call-update) | async-done | bytes 73744 | tf_op jit(solution)/shard_map/reduce_scatter | solution.py:264
  752.0 65.8 %reduce-scatter.28.cloned.1.call-done = f32[96,192]{1,0:T(8,128)} async-done(((f32[768,192]{1,0:T(8,128)}), f32[96,192]{1,0:T(8,128)}) %reduce-scatter.28.cloned.1.call-update) | async-done | bytes 73744 | tf_op jit(solution)/shard_map/reduce_scatter | solution.py:262
  817.8 65.3 %reduce-scatter.26.cloned.1.call-done = f32[96,192]{1,0:T(8,128)} async-done(((f32[768,192]{1,0:T(8,128)}), f32[96,192]{1,0:T(8,128)}) %reduce-scatter.26.cloned.1.call-update) | async-done | bytes 73744 | tf_op jit(solution)/shard_map/reduce_scatter | solution.py:261
  883.1 65.8 %reduce-scatter.24.cloned.1.call-done = f32[96,192]{1,0:T(8,128)} async-done(((f32[768,192]{1,0:T(8,128)}), f32[96,192]{1,0:T(8,128)}) %reduce-scatter.24.cloned.1.call-update) | async-done | bytes 73744 | tf_op jit(solution)/shard_map/reduce_scatter | solution.py:259
  (181 shorter events, 74.6 us)
Async XLA Ops:
  8.0 50.8 %copy-start.31 = (bf16[8,3]{0,1:T(4,128)(2,1)S(1)}, bf16[8,3]{0,1:T(4,128)(2,1)}, u32[]{:S(2)}) copy-start(bf16[8,3]{0,1:T(4,128)(2,1)} %param.22) | copy-start | bytes 148
  8.0 67.6 %copy-start.32 = (bf16[8,3]{0,1:T(4,128)(2,1)S(1)}, bf16[8,3]{0,1:T(4,128)(2,1)}, u32[]{:S(2)}) copy-start(bf16[8,3]{0,1:T(4,128)(2,1)} %param.25) | copy-start | bytes 148
  8.0 85.7 %copy-start.22 = (bf16[96,192]{1,0:T(8,128)(2,1)S(1)}, bf16[96,192]{1,0:T(8,128)(2,1)}, u32[]{:S(2)}) copy-start(bf16[96,192]{1,0:T(8,128)(2,1)} %param.21) | copy-start | bytes 110596
  8.1 116.8 %copy-start.23 = (bf16[96,192]{1,0:T(8,128)(2,1)S(1)}, bf16[96,192]{1,0:T(8,128)(2,1)}, u32[]{:S(2)}) copy-start(bf16[96,192]{1,0:T(8,128)(2,1)} %param.23) | copy-start | bytes 110596
  8.1 147.8 %copy-start.24 = (bf16[96,192]{1,0:T(8,128)(2,1)S(1)}, bf16[96,192]{1,0:T(8,128)(2,1)}, u32[]{:S(2)}) copy-start(bf16[96,192]{1,0:T(8,128)(2,1)} %param.24) | copy-start | bytes 110596
  8.1 178.9 %copy-start.25 = (bf16[96,192]{1,0:T(8,128)(2,1)S(1)}, bf16[96,192]{1,0:T(8,128)(2,1)}, u32[]{:S(2)}) copy-start(bf16[96,192]{1,0:T(8,128)(2,1)} %param.26) | copy-start | bytes 110596
  8.1 209.9 %all-gather.9.cloned.1.call-start = ((), (), s32[]{:S(2)}) async-start(), calls=%async_computation.10 | async-start | bytes 1966080 | tf_op jit(solution)/shard_map/all_gather | solution.py:165
  9.4 49.4 %copy-start.26 = (f32[256]{0:T(256)}, f32[256]{0:T(256)S(1)}, u32[]{:S(2)}) copy-start(f32[256]{0:T(256)S(1)} %broadcast_multiply_fusion.5) | copy-start | bytes 3076
  10.8 48.0 %copy-start.29 = (f32[256]{0:T(256)}, f32[256]{0:T(256)S(1)}, u32[]{:S(2)}) copy-start(f32[256]{0:T(256)S(1)} %add_rsqrt_fusion.1) | copy-start | bytes 3076
  56.6 68.2 %copy-start.20 = (f32[768]{0:T(1024)}, f32[768]{0:T(1024)S(1)}, u32[]{:S(2)}) copy-start(f32[768]{0:T(1024)S(1)} %convert_element_type.132) | copy-start | bytes 9220
  58.8 200.6 %reduce-scatter.16.cloned.1.call-start = ((), (), s32[]{:S(2)}) async-start(), calls=%async_computation.11 | async-start | bytes 1966080 | tf_op jit(solution)/shard_map/reduce_scatter | solution.py:181
  124.8 99.5 %copy-start.12 = (bf16[768,192]{1,0:T(8,128)(2,1)}, bf16[768,192]{1,0:T(8,128)(2,1)S(1)}, u32[]{:S(2)}) copy-start(bf16[768,192]{1,0:T(8,128)(2,1)S(1)} %all_gather.62) | copy-start | bytes 884740
  155.9 68.4 %copy-start.10 = (bf16[768,192]{1,0:T(8,128)(2,1)}, bf16[768,192]{1,0:T(8,128)(2,1)S(1)}, u32[]{:S(2)}) copy-start(bf16[768,192]{1,0:T(8,128)(2,1)S(1)} %all_gather.64) | copy-start | bytes 884740
  187.0 39.4 %copy-start.7 = (bf16[768,192]{1,0:T(8,128)(2,1)}, bf16[768,192]{1,0:T(8,128)(2,1)S(1)}, u32[]{:S(2)}) copy-start(bf16[768,192]{1,0:T(8,128)(2,1)S(1)} %all_gather.60) | copy-start | bytes 884740
  231.3 28.1 %copy-start.2 = (f32[1,256,768]{2,1,0:T(8,128)S(1)}, f32[1,256,768]{2,1,0:T(8,128)}, u32[]{:S(2)}) copy-start(f32[1,256,768]{2,1,0:T(8,128)} %param.17) | copy-start | bytes 2359300
  233.9 62.7 %all-gather.13.cloned.1.call-start = ((), (), s32[]{:S(2)}) async-start(), calls=%async_computation.13 | async-start | bytes 1327104 | tf_op jit(solution)/shard_map/all_gather | solution.py:157
  234.5 62.1 %all-gather.11.cloned.1.call-start = ((), (), s32[]{:S(2)}) async-start(), calls=%async_computation.12 | async-start | bytes 1966080 | tf_op jit(solution)/shard_map/all_gather | solution.py:186
  263.4 76.1 %all-gather.15.cloned.1.call-start = ((), (), s32[]{:S(2)}) async-start(), calls=%async_computation.14 | async-start | bytes 1327104 | tf_op jit(solution)/shard_map/all_gather | solution.py:159
  264.0 95.7 %all-gather.17.cloned.1.call-start = ((), (), s32[]{:S(2)}) async-start(), calls=%async_computation.16 | async-start | bytes 1966080 | tf_op jit(solution)/shard_map/all_gather | solution.py:196
  266.9 130.3 %reduce-scatter.20.cloned.1.call-start = ((), (), s32[]{:S(2)}) async-start(), calls=%async_computation.17 | async-start | bytes 1966080 | tf_op jit(solution)/shard_map/reduce_scatter | solution.py:205
  369.0 58.9 %reduce-scatter.18.cloned.1.call-start = ((), (), s32[]{:S(2)}) async-start(), calls=%async_computation.15 | async-start | bytes 1966080 | tf_op jit(solution)/shard_map/reduce_scatter | solution.py:191
  373.4 79.0 %all-gather.19.cloned.1.call-start = ((), (), s32[]{:S(2)}) async-start(), calls=%async_computation.18 | async-start | bytes 1966080 | tf_op jit(solution)/shard_map/all_gather | solution.py:214
  432.8 141.7 %reduce-scatter.22.cloned.1.call-start = ((), (), s32[]{:S(2)}) async-start(), calls=%async_computation.19 | async-start | bytes 1966080 | tf_op jit(solution)/shard_map/reduce_scatter | solution.py:239
  512.5 107.3 %reduce-scatter.32.cloned.1.call-start = ((), (), s32[]{:S(2)}) async-start(), calls=%async_computation.24 | async-start | bytes 2654208 | tf_op jit(solution)/shard_map/reduce_scatter | solution.py:265
  517.4 169.1 %reduce-scatter.34.cloned.1.call-start = ((), (), s32[]{:S(2)}) async-start(), calls=%async_computation.25 | async-start | bytes 2654208
  525.4 226.6 %reduce-scatter.30.cloned.1.call-start = ((), (), s32[]{:S(2)}) async-start(), calls=%async_computation.23 | async-start | bytes 884736 | tf_op jit(solution)/shard_map/reduce_scatter | solution.py:264
  528.6 289.2 %reduce-scatter.28.cloned.1.call-start = ((), (), s32[]{:S(2)}) async-start(), calls=%async_computation.22 | async-start | bytes 884736 | tf_op jit(solution)/shard_map/reduce_scatter | solution.py:262
  530.2 44.3 %copy-start.21 = (f32[768]{0:T(1024)S(1)}, f32[768]{0:T(1024)}, u32[]{:S(2)}) copy-start(f32[768]{0:T(1024)} %copy-done.20) | copy-start | bytes 9220
  530.3 44.3 %copy-start.27 = (f32[256]{0:T(256)S(1)}, f32[256]{0:T(256)}, u32[]{:S(2)}) copy-start(f32[256]{0:T(256)} %copy-done.26) | copy-start | bytes 3076
  530.3 352.8 %reduce-scatter.26.cloned.1.call-start = ((), (), s32[]{:S(2)}) async-start(), calls=%async_computation.21 | async-start | bytes 884736 | tf_op jit(solution)/shard_map/reduce_scatter | solution.py:261
  531.9 85.8 %copy-start.4 = (f32[1,256,768]{2,1,0:T(8,128)S(1)}, f32[1,256,768]{2,1,0:T(8,128)}, u32[]{:S(2)}) copy-start(f32[1,256,768]{2,1,0:T(8,128)} %copy-done.3) | copy-start | bytes 2359300
  531.9 416.9 %reduce-scatter.24.cloned.1.call-start = ((), (), s32[]{:S(2)}) async-start(), calls=%async_computation.20 | async-start | bytes 884736 | tf_op jit(solution)/shard_map/reduce_scatter | solution.py:259
  (19 other events, 94.4 us)
Sparse Core Ops, SparseCore 0:
  58.9 16.9 all-gather.8
  234.0 25.3 reduce-scatter.15
  369.1 28.1 reduce-scatter.19
  399.6 28.1 reduce-scatter.17
Sparse Core Ops, SparseCore 1:
  236.8 38.7 all-gather.12
  277.6 18.0 all-gather.10
  297.9 41.5 all-gather.14
  341.7 18.0 all-gather.16
  432.9 19.5 all-gather.18
  512.6 28.1 reduce-scatter.21
  544.7 69.7 reduce-scatter.31
  618.4 68.0 reduce-scatter.33
  690.3 61.7 reduce-scatter.29
  756.2 61.5 reduce-scatter.27
  821.5 61.5 reduce-scatter.25
  887.3 61.5 reduce-scatter.23
where the time goes:
time: 966 us; the launch traced here: 956 us
  waiting for transfers between devices  481 us (50%)
  blocking collectives  299 us (31%)
  matrix products  106 us (11%)
  other arithmetic  26.7 us (3%)
  local copies, waits for them, and re-layouts  24.5 us (3%)
  between operations  17.6 us (2%)
    unnamed x3, blocking collectives  115 us
    unnamed x17, waiting for transfers between devices  67.7 us
    reduce_scatter x1, waiting for transfers between devices, on_device(): lax.psum_scatter(value_grad_part, 'dp', scatter_dimension=0, tiled=True)  65.8 us
    reduce_scatter x1, waiting for transfers between devices, on_device(): lax.psum_scatter(query_grad_part, 'dp', scatter_dimension=0, tiled=True)  65.8 us
    reduce_scatter x1, waiting for transfers between devices, on_device(): lax.psum_scatter(output_grad, 'dp', scatter_dimension=0, tiled=True)  65.5 us
    reduce_scatter x1, waiting for transfers between devices, on_device(): lax.psum_scatter(key_grad_part, 'dp', scatter_dimension=0, tiled=True)  65.3 us
    all_gather x1, waiting for transfers between devices, on_device(): lax.all_gather(outer_weight, 'dp', axis=0, tiled=True)  37.4 us
    dot_general x12, matrix products, matmul(): return jnp.dot(left, right, preferred_element_type=jnp.float32)  31.2 us
  transfers between devices with their start and end apart: 16, of which 11 were waited for; matrix products, arithmetic and copies ran while one was open for 6% of the time, Pallas kernels for 0%

commit v1 on v0

v1 whole, which is shorter than its diff:
```python
import functools
import math

import jax
import jax.numpy as jnp
from jax import lax
from jax.experimental import pallas as pl
from jax.experimental.pallas import tpu as pltpu
from jax.sharding import PartitionSpec as P

HD = 64
EPS = 1e-05
ROOT_HALF = 0.7071067811865476
DENSITY_NORM = 0.3989422804014327
MESH = pl.DeviceIdType.MESH
CHUNK = 64
VROWS = 8
F32 = jnp.float32
BF16 = jnp.bfloat16


def gelu_value(preact):
    return 0.5 * preact * (1.0 + lax.erf(preact * ROOT_HALF))


def gelu_slope(preact):
    return 0.5 * (1.0 + lax.erf(preact * ROOT_HALF)) + preact * DENSITY_NORM * jnp.exp(
        -0.5 * preact * preact
    )


def matmul(left, right):
    return jnp.dot(left, right, preferred_element_type=F32)


def matmul_nt(left, right):
    return lax.dot_general(left, right, (((1,), (1,)), ((), ())), preferred_element_type=F32)


def split_heads(block):
    return block.reshape(block.shape[0], block.shape[1] // HD, HD)


def places():
    d = lax.axis_index("dp")
    t = lax.axis_index("tensor")
    sib = t + 1 - 2 * lax.rem(t, 2)
    opp = lax.rem(t + 2, 4)
    diag = lax.rem(sib + 2, 4)
    return d, t, sib, opp, diag


def greet(dp, tensor_peers):
    d, t = lax.axis_index("dp"), lax.axis_index("tensor")
    barrier = pltpu.get_barrier_semaphore()
    for peer in tensor_peers:
        pl.semaphore_signal(barrier, inc=1, device_id=(d, peer), device_id_type=MESH)

    def signal(k, carry):
        pl.semaphore_signal(
            barrier, inc=1, device_id=(lax.rem(d + k, dp), t), device_id_type=MESH
        )
        return carry

    if dp > 1:
        lax.fori_loop(1, dp, signal, 0)
    pl.semaphore_wait(barrier, len(tensor_peers) + dp - 1)


def normed_rows(block):
    row_mean = jnp.mean(block, axis=-1, keepdims=True)
    centred = block - row_mean
    rstd = lax.rsqrt(jnp.mean(centred * centred, axis=-1, keepdims=True) + EPS)
    return centred * rstd, rstd


def norm_back(gradient, normed, rstd, gain):
    scaled = gradient * gain
    first = jnp.mean(scaled, axis=-1, keepdims=True)
    second = jnp.mean(scaled * normed, axis=-1, keepdims=True)
    return (scaled - first - normed * second) * rstd


def rows_of(c):
    return pl.ds(c * CHUNK, CHUNK)


class Gather:
    def __init__(self, buf, send, recv):
        self.buf, self.send, self.recv = buf, send, recv
        self.chunks = buf.shape[1] // CHUNK

    def copy(self, slot, kind, c, peer):
        d = lax.axis_index("dp")
        ref = self.buf.at[slot, rows_of(c)]
        return pltpu.make_async_remote_copy(
            src_ref=ref,
            dst_ref=ref,
            send_sem=self.send.at[kind, c],
            recv_sem=self.recv.at[kind, c],
            device_id=(d, peer),
            device_id_type=MESH,
        )

    def start(self, c):
        _, t, sib, opp, _ = places()
        self.copy(t, 1, c, opp).start()
        self.copy(t, 0, c, sib).start()

    def forward(self, c):
        _, t, sib, opp, _ = places()
        self.copy(opp, 1, c, opp).wait_recv()
        self.copy(opp, 2, c, sib).start()

    def finish(self):
        _, t, sib, opp, diag = places()
        for c in range(self.chunks):
            self.copy(sib, 0, c, sib).wait_recv()
            self.copy(diag, 2, c, sib).wait_recv()
        for c in range(self.chunks):
            self.copy(t, 0, c, sib).wait_send()
            self.copy(t, 1, c, opp).wait_send()
            self.copy(opp, 2, c, sib).wait_send()


class Scatter:
    def __init__(self, part, near, total, far, send, recv):
        self.part, self.near, self.total, self.far = part, near, total, far
        self.send, self.recv = send, recv
        self.chunks = part.shape[1] // CHUNK

    def copy(self, src, dst, kind, c, peer):
        d = lax.axis_index("dp")
        return pltpu.make_async_remote_copy(
            src_ref=src,
            dst_ref=dst,
            send_sem=self.send.at[kind, c],
            recv_sem=self.recv.at[kind, c],
            device_id=(d, peer),
            device_id_type=MESH,
        )

    def to_sibling(self, kind, c):
        _, _, sib, _, diag = places()
        block = sib if kind == 0 else diag
        return self.copy(
            self.part.at[block, rows_of(c)], self.near.at[kind, rows_of(c)], kind, c, sib
        )

    def across(self, c):
        _, _, _, opp, _ = places()
        return self.copy(self.total.at[rows_of(c)], self.far.at[rows_of(c)], 2, c, opp)

    def start(self):
        for c in range(self.chunks):
            self.to_sibling(1, c).start()
        for c in range(self.chunks):
            self.to_sibling(0, c).start()

    def middle(self, c):
        _, _, _, opp, _ = places()
        self.to_sibling(1, c).wait_recv()
        rows = rows_of(c)
        self.total[rows, :] = (
            self.part[opp, rows, :].astype(F32) + self.near[1, rows, :].astype(F32)
        ).astype(BF16)
        self.across(c).start()

    def result(self, c):
        _, t, _, _, _ = places()
        self.to_sibling(0, c).wait_recv()
        self.across(c).wait_recv()
        rows = rows_of(c)
        return (
            self.part[t, rows, :].astype(F32)
            + self.near[0, rows, :].astype(F32)
            + self.far[rows, :].astype(F32)
        )

    def finish(self):
        for c in range(self.chunks):
            self.to_sibling(0, c).wait_send()
            self.to_sibling(1, c).wait_send()
            self.across(c).wait_send()


def scatter_scratch(rows, width):
    return [
        pltpu.VMEM((2, rows, width), BF16),
        pltpu.VMEM((rows, width), BF16),
        pltpu.VMEM((rows, width), BF16),
        pltpu.SemaphoreType.DMA((3, rows // CHUNK)),
        pltpu.SemaphoreType.DMA((3, rows // CHUNK)),
    ]


def gather_scratch(rows):
    return [
        pltpu.SemaphoreType.DMA((3, rows // CHUNK)),
        pltpu.SemaphoreType.DMA((3, rows // CHUNK)),
    ]


def dp_copy(dp, k, src, dst, send, recv):
    d, t = lax.axis_index("dp"), lax.axis_index("tensor")
    return pltpu.make_async_remote_copy(
        src_ref=src,
        dst_ref=dst,
        send_sem=send.at[k],
        recv_sem=recv.at[k],
        device_id=(lax.rem(d + k, dp), t),
        device_id_type=MESH,
    )


def each_peer(dp, body):
    def step(k, carry):
        body(k)
        return carry

    lax.fori_loop(1, dp, step, 0)


def first_kernel(
    dp, x_ref, cot_ref, small_ref, pack_ref,
    gathered_ref, vec_ref, low_ref, cot_all_ref,
    small_buf, s_send, s_recv, w_send, w_recv, own_sem, l_send, l_recv, c_send, c_recv,
):
    d, t, sib, opp, diag = places()
    own = pltpu.make_async_copy(pack_ref, gathered_ref.at[d], own_sem)
    own.start()
    small_buf[d] = small_ref[...]
    greet(dp, (sib, opp))

    def small_copy(k):
        return dp_copy(dp, k, small_buf.at[d], small_buf.at[d], s_send, s_recv)

    def pack_copy(k):
        return dp_copy(dp, k, pack_ref, gathered_ref.at[d], w_send, w_recv)

    each_peer(dp, lambda k: small_copy(k).start())
    each_peer(dp, lambda k: pack_copy(k).start())
    low = Gather(low_ref, l_send, l_recv)
    cot = Gather(cot_all_ref, c_send, c_recv)
    each_peer(dp, lambda k: small_copy(k).wait_recv())
    vec_ref[...] = jnp.sum(small_buf[...], axis=0)
    gain, shift = vec_ref[0:1, :], vec_ref[1:2, :]
    for c in range(low.chunks):
        normed, _ = normed_rows(x_ref[rows_of(c), :])
        low_ref[t, rows_of(c), :] = (normed * gain + shift).astype(BF16)
        low.start(c)
    for c in range(cot.chunks):
        cot_all_ref[t, rows_of(c), :] = cot_ref[rows_of(c), :].astype(BF16)
        cot.start(c)
    for c in range(low.chunks):
        low.forward(c)
    for c in range(cot.chunks):
        cot.forward(c)
    low.finish()
    cot.finish()
    each_peer(dp, lambda k: small_copy(k).wait_send())
    each_peer(dp, lambda k: pack_copy(k).wait())
    own.wait()


def second_kernel(
    part_ref, x_ref, vec_ref,
    mixed_ref, low_ref,
    near, total, far, r_send, r_recv, l_send, l_recv,
):
    d, t, sib, opp, diag = places()
    greet(1, (sib, opp))
    scat = Scatter(part_ref, near, total, far, r_send, r_recv)
    low = Gather(low_ref, l_send, l_recv)
    scat.start()
    for c in range(scat.chunks):
        scat.middle(c)
    bias, gain, shift = vec_ref[2:3, :], vec_ref[3:4, :], vec_ref[4:5, :]
    for c in range(scat.chunks):
        mixed = x_ref[rows_of(c), :] + scat.result(c) + bias
        mixed_ref[rows_of(c), :] = mixed
        normed, _ = normed_rows(mixed)
        low_ref[t, rows_of(c), :] = (normed * gain + shift).astype(BF16)
        low.start(c)
    for c in range(low.chunks):
        low.forward(c)
    low.finish()
    scat.finish()


def third_kernel(
    npart_ref, fpart_ref, mixed_ref, cot_ref, vec_ref,
    grad_ref, all_ref, out_ref, sums_ref,
    n_near, n_total, n_far, n_send, n_recv,
    f_near, f_total, f_far, f_send, f_recv,
    g_send, g_recv,
):
    d, t, sib, opp, diag = places()
    greet(1, (sib, opp))
    first = Scatter(npart_ref, n_near, n_total, n_far, n_send, n_recv)
    feed = Scatter(fpart_ref, f_near, f_total, f_far, f_send, f_recv)
    gather = Gather(all_ref, g_send, g_recv)
    first.start()
    for c in range(first.chunks):
        first.middle(c)
    feed.start()
    gain = vec_ref[3:4, :]
    sums = [jnp.zeros_like(gain) for _ in range(4)]
    for c in range(first.chunks):
        gradient = first.result(c)
        cot = cot_ref[rows_of(c), :]
        normed, rstd = normed_rows(mixed_ref[rows_of(c), :])
        mixed_grad = cot + norm_back(gradient, normed, rstd, gain)
        grad_ref[rows_of(c), :] = mixed_grad
        all_ref[t, rows_of(c), :] = mixed_grad.astype(BF16)
        gather.start(c)
        terms = (mixed_grad, gradient * normed, gradient, cot)
        sums = [s + jnp.sum(v, axis=0, keepdims=True) for s, v in zip(sums, terms)]
    zero = jnp.zeros_like(gain)
    sums_ref[...] = jnp.concatenate([zero, zero] + sums + [zero, zero], axis=0)
    for c in range(feed.chunks):
        feed.middle(c)
    for c in range(gather.chunks):
        gather.forward(c)
    bias = vec_ref[5:6, :]
    for c in range(feed.chunks):
        out_ref[rows_of(c), :] = mixed_ref[rows_of(c), :] + feed.result(c) + bias
    gather.finish()
    first.finish()
    feed.finish()


def fourth_kernel(
    dp, part_ref, x_ref, mixed_grad_ref, vec_ref, sums_ref, wgrad_ref,
    input_grad_ref, wout_ref, vout_ref,
    near, total, far, r_send, r_recv,
    landed, w_send, w_recv, group, t_send, t_recv, whole, v_send, v_recv,
):
    d, t, sib, opp, diag = places()
    greet(dp, (sib, opp, diag))
    scat = Scatter(part_ref, near, total, far, r_send, r_recv)
    scat.start()

    def weight_copy(k):
        return dp_copy(
            dp, k, wgrad_ref.at[lax.rem(d + k, dp)], landed.at[d], w_send, w_recv
        )

    each_peer(dp, lambda k: weight_copy(k).start())
    for c in range(scat.chunks):
        scat.middle(c)
    gain = vec_ref[0:1, :]
    sums = [jnp.zeros_like(gain) for _ in range(2)]
    for c in range(scat.chunks):
        gradient = scat.result(c)
        normed, rstd = normed_rows(x_ref[rows_of(c), :])
        input_grad_ref[rows_of(c), :] = mixed_grad_ref[rows_of(c), :] + norm_back(
            gradient, normed, rstd, gain
        )
        terms = (gradient * normed, gradient)
        sums = [s + jnp.sum(v, axis=0, keepdims=True) for s, v in zip(sums, terms)]
    mine = sums_ref[...] + jnp.concatenate(
        sums + [jnp.zeros((VROWS - 2, gain.shape[1]), F32)], axis=0
    )
    group[t] = mine
    tensor_copies = [
        pltpu.make_async_remote_copy(
            src_ref=group.at[t],
            dst_ref=group.at[t],
            send_sem=t_send.at[i],
            recv_sem=t_recv.at[i],
            device_id=(d, peer),
            device_id_type=MESH,
        )
        for i, peer in enumerate((sib, opp, diag))
    ]
    for copy in tensor_copies:
        copy.start()
    for copy in tensor_copies:
        copy.wait()
    over_group = jnp.sum(group[...], axis=0)
    row = lax.broadcasted_iota(jnp.int32, mine.shape, 0)
    whole[d] = jnp.where(row < 6, over_group, mine)

    def vector_copy(k):
        return dp_copy(dp, k, whole.at[d], whole.at[d], v_send, v_recv)

    each_peer(dp, lambda k: vector_copy(k).start())
    landed[d] = wgrad_ref[d]
    each_peer(dp, lambda k: weight_copy(k).wait())
    acc = landed[0].astype(F32)
    for k in range(1, dp):
        acc = acc + landed[k].astype(F32)
    wout_ref[...] = acc
    each_peer(dp, lambda k: vector_copy(k).wait())
    vout_ref[...] = jnp.sum(whole[...], axis=0)
    scat.finish()


VM = pl.BlockSpec(memory_space=pltpu.VMEM)
ANY = pl.BlockSpec(memory_space=pl.ANY)


def comm_call(kernel, ident, in_specs, outs, out_specs, scratch, flops=20_000_000_000):
    return pl.pallas_call(
        kernel,
        out_shape=tuple(jax.ShapeDtypeStruct(s, dt) for s, dt in outs),
        in_specs=in_specs,
        out_specs=tuple(out_specs),
        scratch_shapes=scratch,
        cost_estimate=pl.CostEstimate(flops=flops, bytes_accessed=4_000_000, transcendentals=0),
        compiler_params=pltpu.CompilerParams(
            collective_id=ident, has_side_effects=True, vmem_limit_bytes=36 * 1024 * 1024
        ),
    )


def token_kernel(a_ref, b_ref, o_ref):
    o_ref[...] = lax.dot_general(
        a_ref[...], b_ref[...], (((0,), (0,)), ((), ())), preferred_element_type=F32
    ).astype(o_ref.dtype)


def token_product(left, right):
    tokens, m = left.shape
    n = right.shape[1]
    tile = 256
    return pl.pallas_call(
        token_kernel,
        grid=(m // tile,),
        out_shape=jax.ShapeDtypeStruct((m, n), BF16),
        in_specs=[
            pl.BlockSpec((tokens, tile), lambda i: (0, i)),
            pl.BlockSpec((tokens, n), lambda i: (0, 0)),
        ],
        out_specs=pl.BlockSpec((tile, n), lambda i: (i, 0)),
        cost_estimate=pl.CostEstimate(
            flops=2 * tokens * m * n, bytes_accessed=2 * (tokens * (m + n) + m * n), transcendentals=0
        ),
        compiler_params=pltpu.CompilerParams(vmem_limit_bytes=24 * 1024 * 1024),
    )(left, right)


def attend(operands):
    queries, key_rows, values = operands
    score_scale = 1.0 / math.sqrt(HD)
    scores = (
        jnp.einsum(
            "qhd,khd->hqk",
            split_heads(queries),
            split_heads(key_rows),
            preferred_element_type=jnp.float32,
        )
        * score_scale
    )
    row_max = jnp.max(scores, axis=-1, keepdims=True)
    log_total = row_max + jnp.log(jnp.sum(jnp.exp(scores - row_max), axis=-1, keepdims=True))
    prob_low = jnp.exp(scores - log_total).astype(jnp.bfloat16)
    context = jnp.einsum(
        "hqk,khd->qhd", prob_low, split_heads(values), preferred_element_type=jnp.float32
    )
    return (context.reshape(queries.shape).astype(jnp.bfloat16), log_total)


def attend_back(operands):
    queries, key_rows, values, context_grad, log_total = operands
    score_scale = 1.0 / math.sqrt(HD)
    query_heads = split_heads(queries)
    key_heads = split_heads(key_rows)
    grad_heads = split_heads(context_grad)
    scores = (
        jnp.einsum("qhd,khd->hqk", query_heads, key_heads, preferred_element_type=jnp.float32)
        * score_scale
    )
    prob_full = jnp.exp(scores - log_total)
    prob_low = prob_full.astype(jnp.bfloat16)
    value_grad = jnp.einsum(
        "hqk,qhd->khd", prob_low, grad_heads, preferred_element_type=jnp.float32
    )
    prob_grad = jnp.einsum(
        "qhd,khd->hqk", grad_heads, split_heads(values), preferred_element_type=jnp.float32
    )
    row_dot = jnp.sum(prob_full * prob_grad, axis=-1, keepdims=True)
    score_grad = (prob_full * (prob_grad - row_dot) * score_scale).astype(jnp.bfloat16)
    query_grad = jnp.einsum(
        "hqk,khd->qhd", score_grad, key_heads, preferred_element_type=jnp.float32
    )
    key_low = jnp.einsum(
        "hqk,qhd->khd", score_grad, query_heads, preferred_element_type=jnp.float32
    ).astype(jnp.bfloat16)
    return (
        query_grad.reshape(queries.shape),
        key_low.reshape(queries.shape),
        value_grad.reshape(queries.shape),
    )


def on_device(
    dp,
    layer_input,
    out_cotangent,
    mix_gain,
    mix_shift,
    query_weight,
    query_bias,
    key_weight,
    value_weight,
    value_bias,
    output_weight,
    output_bias,
    feed_gain,
    feed_shift,
    inner_weight,
    inner_bias,
    outer_weight,
    outer_bias,
):
    d = lax.axis_index("dp")
    t = lax.axis_index("tensor")
    clips, share, feats = layer_input.shape
    rows = clips * share
    frames = share * 4
    width = query_weight.shape[1]
    shard = query_weight.shape[0]
    hidden_units = inner_weight.shape[1]

    inner_full = lax.all_gather(inner_weight, "dp", axis=0, tiled=True)
    outer_full = lax.all_gather(outer_weight, "dp", axis=0, tiled=True)

    def placed_bias(bias):
        full = jnp.zeros((HD, bias.shape[1]), F32)
        full = lax.dynamic_update_slice(full, bias.astype(F32), (d * bias.shape[0], 0))
        return full.T.reshape(-1)

    vectors = jnp.stack([mix_gain, mix_shift, output_bias, feed_gain, feed_shift, outer_bias])
    upper = lax.dynamic_update_slice(
        jnp.zeros((6, feats), F32), vectors.astype(F32), (0, d * vectors.shape[1])
    )
    none = jnp.zeros((width,), F32)
    head_row = jnp.concatenate([placed_bias(query_bias), none, placed_bias(value_bias), none])
    small = jnp.concatenate([upper, head_row[None], placed_bias(inner_bias)[None]], axis=0)
    pack = jnp.concatenate([query_weight, key_weight, value_weight, output_weight], axis=1)

    x = layer_input.reshape(rows, feats)
    cot = out_cotangent.reshape(rows, feats)
    block = (4, rows, feats)

    def to_tokens(gathered):
        return (
            gathered.reshape(4, clips, share, feats)
            .transpose(1, 0, 2, 3)
            .reshape(clips * frames, feats)
        )

    def to_blocks(tokens):
        return (
            tokens.astype(BF16)
            .reshape(clips, 4, share, feats)
            .transpose(1, 0, 2, 3)
            .reshape(block)
        )

    gathered_pack, vec, low_one, cot_all = comm_call(
        functools.partial(first_kernel, dp),
        1,
        [VM, VM, VM, ANY],
        [((dp,) + pack.shape, BF16), ((VROWS, feats), F32), (block, BF16), (block, BF16)],
        [ANY, VM, VM, VM],
        [
            pltpu.VMEM((dp, VROWS, feats), F32),
            pltpu.SemaphoreType.DMA((dp,)),
            pltpu.SemaphoreType.DMA((dp,)),
            pltpu.SemaphoreType.DMA((dp,)),
            pltpu.SemaphoreType.DMA((dp,)),
            pltpu.SemaphoreType.DMA,
        ]
        + gather_scratch(rows)
        + gather_scratch(rows),
    )(x, cot, small, pack)
    flat_one = to_tokens(low_one)
    cot_tokens = to_tokens(cot_all)
    attn_weights = gathered_pack.reshape(feats, 4 * width)
    qkv_full = attn_weights[:, : 3 * width]
    output_full = attn_weights[:, 3 * width :]
    qkv = (matmul(flat_one, qkv_full) + vec[6, : 3 * width]).astype(BF16)
    clip_qkv = qkv.reshape(clips, frames, 3 * width)
    clip_queries = clip_qkv[:, :, :width]
    clip_keys = clip_qkv[:, :, width : 2 * width]
    clip_values = clip_qkv[:, :, 2 * width :]
    context, log_total = lax.map(attend, (clip_queries, clip_keys, clip_values))
    flat_context = context.reshape(clips * frames, width)
    attn_part = to_blocks(matmul_nt(flat_context, output_full))

    mixed, low_two = comm_call(
        second_kernel,
        2,
        [VM, VM, VM],
        [((rows, feats), F32), (block, BF16)],
        [VM, VM],
        scatter_scratch(rows, feats) + gather_scratch(rows),
    )(attn_part, x, vec)
    flat_two = to_tokens(low_two)
    preact = matmul(flat_two, inner_full) + vec[7, :hidden_units]
    hidden = gelu_value(preact).astype(BF16)
    preact_grad = matmul(cot_tokens, outer_full) * gelu_slope(preact)
    preact_low = preact_grad.astype(BF16)
    inner_bias_sum = jnp.sum(preact_grad, axis=0)
    norm_two_part = to_blocks(matmul_nt(preact_low, inner_full))
    feed_part = to_blocks(matmul_nt(hidden, outer_full))

    outer_part = token_product(cot_tokens, hidden)
    inner_part = token_product(flat_two, preact_low)
    inner_weight_grad = lax.psum_scatter(inner_part, "dp", scatter_dimension=0, tiled=True)
    outer_weight_grad = lax.psum_scatter(outer_part, "dp", scatter_dimension=0, tiled=True)

    mixed_grad, mixed_all, layer_output, sums = comm_call(
        third_kernel,
        3,
        [VM] * 5,
        [((rows, feats), F32), (block, BF16), ((rows, feats), F32), ((VROWS, feats), F32)],
        [VM] * 4,
        scatter_scratch(rows, feats) + scatter_scratch(rows, feats) + gather_scratch(rows),
    )(norm_two_part, feed_part, mixed, cot, vec)
    mixed_tokens = to_tokens(mixed_all)
    output_part = token_product(mixed_tokens, flat_context)
    context_grad = matmul(mixed_tokens, output_full).astype(BF16).reshape(clips, frames, width)
    query_grad, key_low, value_grad = lax.map(
        attend_back, (clip_queries, clip_keys, clip_values, context_grad, log_total)
    )
    query_grad = query_grad.reshape(clips * frames, width)
    key_low = key_low.reshape(clips * frames, width)
    value_grad = value_grad.reshape(clips * frames, width)
    low_grads = jnp.concatenate(
        [query_grad.astype(BF16), key_low, value_grad.astype(BF16)], axis=1
    )
    norm_one_part = to_blocks(matmul_nt(low_grads, qkv_full))
    attn_wpart = jnp.concatenate([token_product(flat_one, low_grads), output_part], axis=1)
    bias_row = jnp.concatenate(
        [jnp.sum(query_grad, axis=0), none, jnp.sum(value_grad, axis=0), none]
    )
    sums = sums + jnp.concatenate(
        [jnp.zeros((VROWS - 2, feats), F32), bias_row[None], inner_bias_sum[None]], axis=0
    )

    input_grad, attn_grads, vector_sums = comm_call(
        functools.partial(fourth_kernel, dp),
        4,
        [VM] * 6,
        [((rows, feats), F32), ((shard, 4 * width), F32), ((VROWS, feats), F32)],
        [VM] * 3,
        scatter_scratch(rows, feats)
        + [
            pltpu.VMEM((dp, shard, 4 * width), BF16),
            pltpu.SemaphoreType.DMA((dp,)),
            pltpu.SemaphoreType.DMA((dp,)),
            pltpu.VMEM((4, VROWS, feats), F32),
            pltpu.SemaphoreType.DMA((3,)),
            pltpu.SemaphoreType.DMA((3,)),
            pltpu.VMEM((dp, VROWS, feats), F32),
            pltpu.SemaphoreType.DMA((dp,)),
            pltpu.SemaphoreType.DMA((dp,)),
        ],
    )(norm_one_part, x, mixed_grad, vec, sums, attn_wpart.reshape(dp, shard, 4 * width))

    piece = feats // (4 * dp)
    mine = lax.dynamic_slice(vector_sums, (0, (d * 4 + t) * piece), (VROWS, piece))

    def bias_share(vector, like):
        table = vector.reshape(-1, HD).T
        return lax.dynamic_slice(table, (d * like.shape[0], 0), like.shape)

    return (
        layer_output.reshape(layer_input.shape),
        input_grad.reshape(layer_input.shape),
        mine[0],
        mine[1],
        attn_grads[:, :width],
        bias_share(vector_sums[6, :width], query_bias),
        attn_grads[:, width : 2 * width],
        attn_grads[:, 2 * width : 3 * width],
        bias_share(vector_sums[6, 2 * width : 3 * width], value_bias),
        attn_grads[:, 3 * width :],
        mine[2],
        mine[3],
        mine[4],
        inner_weight_grad.astype(F32),
        bias_share(vector_sums[7, :hidden_units], inner_bias),
        outer_weight_grad.astype(F32),
        mine[5],
    )


def solution(mesh):
    placed = (
        P("dp", "tensor", None),
        P("dp", "tensor", None),
        P("dp"),
        P("dp"),
        P("dp", "tensor"),
        P("dp", "tensor"),
        P("dp", "tensor"),
        P("dp", "tensor"),
        P("dp", "tensor"),
        P("dp", "tensor"),
        P("dp"),
        P("dp"),
        P("dp"),
        P("dp", "tensor"),
        P("dp", "tensor"),
        P("dp", "tensor"),
        P("dp"),
    )
    return jax.shard_map(
        functools.partial(on_device, mesh.shape["dp"]),
        mesh=mesh,
        in_specs=placed,
        out_specs=(
            P("dp", "tensor", None),
            P("dp", "tensor", None),
            P(("dp", "tensor")),
            P(("dp", "tensor")),
            P("dp", "tensor"),
            P("dp", "tensor"),
            P("dp", "tensor"),
            P("dp", "tensor"),
            P("dp", "tensor"),
            P("dp", "tensor"),
            P(("dp", "tensor")),
            P(("dp", "tensor")),
            P(("dp", "tensor")),
            P("dp", "tensor"),
            P("dp", "tensor"),
            P("dp", "tensor"),
            P(("dp", "tensor")),
        ),
        check_vma=False,
    )
```

time: 966 us -> 314 us (0.33)
  waiting for transfers between devices: 481 us -> 43.4 us
  blocking collectives: 299 us -> 0 us
  Pallas kernels: 0 us -> 141 us
  matrix products: 106 us -> 77.4 us
  other arithmetic: 26.7 us -> 10.1 us
    reduce_scatter x9 -> x2, waiting for transfers between devices: 336 us -> 27.2 us  [the longest x1 27.2 us: on_device(): lax.psum_scatter(inner_part, 'dp', scatter_dimension=0, tiled=True)]
    all_gather x7 -> x0, blocking collectives: 185 us -> none  [the longest x1 31.1 us: on_device(): lax.all_gather(value_weight, 'dp', axis=0, tiled=True)]
    pallas_call x0 -> x8, Pallas kernels: none -> 141 us  [the longest x1 47 us: on_device(): comm_call(functools.partial(fourth_kernel, dp), 4, [VM] * 6, [((rows, fea...]
    unnamed x3 -> x0, blocking collectives: 115 us -> none
    unnamed x17 -> x4, waiting for transfers between devices: 67.7 us -> 1.41 us
    all_gather x6 -> x2, waiting for transfers between devices: 77.2 us -> 14.9 us  [the longest x1 14.9 us: on_device(): outer_full = lax.all_gather(outer_weight, 'dp', axis=0, tiled=True)]
    dot_general x18 -> x8, matrix products: 48.3 us -> 23.4 us  [the longest x4 13.1 us: matmul(): return jnp.dot(left, right, preferred_element_type=F32)]
    reduce_sum x8 -> x0, other arithmetic: 13.6 us -> none  [the longest x1 3.27 us: on_device(): output_bias_part = jnp.sum(mixed_grad, axis=(0, 1))]
  transfers between devices with their start and end apart: 16 -> 4, of which waited for: 11 -> 2; matrix products, arithmetic and copies ran while one was open for 6% -> 30% of each run, Pallas kernels for 0% -> 45%
where the time goes in v1:
time: 314 us; the launch traced here: 313 us
  Pallas kernels  141 us (45%)
  matrix products  77.4 us (25%)
  waiting for transfers between devices  43.4 us (14%)
  local copies, waits for them, and re-layouts  26.4 us (8%)
  between operations  14.3 us (5%)
  other arithmetic  10.1 us (3%)
    pallas_call x1, Pallas kernels, on_device(): comm_call(functools.partial(fourth_kernel, dp), 4, [VM] * 6, [((rows, fea...  47 us
    pallas_call x1, Pallas kernels, on_device(): comm_call(functools.partial(first_kernel, dp), 1, [VM, VM, VM, ANY], [((d...  34 us
    pallas_call x1, Pallas kernels, on_device(): comm_call(third_kernel, 3, [VM] * 5, [((rows, feats), F32), (block, BF16)...  30.3 us
    reduce_scatter x1, waiting for transfers between devices, on_device(): lax.psum_scatter(inner_part, 'dp', scatter_dimension=0, tiled=True)  27.2 us
    pallas_call x1, Pallas kernels, on_device(): comm_call(second_kernel, 2, [VM, VM, VM], [((rows, feats), F32), (block,...  21.8 us
    dot_general x1, matrix products, attend_back(): jnp.einsum('hqk,khd->qhd', score_grad, key_heads, preferred_element_type=...  19.7 us
    dot_general x1, matrix products, attend_back(): jnp.einsum('hqk,qhd->khd', score_grad, query_heads, preferred_element_typ...  19.5 us
    unnamed x69, local copies, waits for them, and re-layouts  15.2 us
  transfers between devices with their start and end apart: 4, of which 2 were waited for; matrix products, arithmetic and copies ran while one was open for 30% of the time, Pallas kernels for 45%

profile of v1, /device:TPU:0, one launch (start us, length us, event | category | flops | bytes accessed | tf_op | source)
XLA Modules:
  0.0 313.2 jit_solution(2127702420735742503)
XLA Ops:
  15.8 34.0 %shard_map.296 = (bf16[8,96,768]{2,1,0:T(8,128)(2,1)S(1)}, f32[8,768]{1,0:T(8,128)S(1)}, bf16[4,256,768]{2,1,0:T(8,128)(2,1)S(1)}, bf16[4,256,768]{2,1,0:T(8,128)(2,1)S(1)}) custom-call(f32[256,768]{1,0:T(8,128)S(1)} %bitcast.92, f32[256,768]{1,0:T(8,128)S(1)} %bitcast.90, f32[8,768]{1,0:T(8,128)S(1)} %pad_maximum_fusion.3.small_ref, ...), custom_call_target="tpu_custom_call" | custom-call | flops 20000000000 | bytes 4000000 | tf_op jit(solution)/shard_map/pallas_call | solution.py:563
  51.6 1.9 multiply_reduce_fusion.1
  53.5 2.1 exponential_reduce_fusion
  55.6 2.2 convolution_convert_fusion.5
  59.0 1.8 convolution_convert_fusion.3
  61.9 21.8 %shard_map.297 = (f32[256,768]{1,0:T(8,128)S(1)}, bf16[4,256,768]{2,1,0:T(8,128)(2,1)S(1)}) custom-call(bf16[4,256,768]{2,1,0:T(8,128)(2,1)S(1)} %bitcast.80, f32[256,768]{1,0:T(8,128)S(1)} %bitcast.93, f32[8,768]{1,0:T(8,128)S(1)} %get-tuple-element.78.vec_ref), custom_call_target="tpu_custom_call" | custom-call | flops 20000000000 | bytes 4000000 | tf_op jit(solution)/shard_map/pallas_call | solution.py:594
  85.8 5.0 %multiply_convert_fusion.1 = (bf16[1024,768]{1,0:T(8,128)(2,1)S(1)}, f32[1024,768]{1,0:T(8,128)}) fusion(f32[768]{0:T(1024)S(1)} %slice_reduce_fusion.1, bf16[1024,768]{1,0:T(8,128)(2,1)} %bitcast.95, bf16[768,768]{1,0:T(8,128)(2,1)} %all-gather.5.cloned.1.call-done), kind=kOutput, calls=%fused_computation.19 | convolution fusion | flops 1212678144 | bytes 7474176 | tf_op jit(solution)/shard_map/dot_general | solution.py:33
  90.8 1.2 copy-done.16
  92.0 2.9 shard_map.303
  94.8 14.9 %all-gather.3.cloned.1.call-done = bf16[768,768]{1,0:T(8,128)(2,1)} async-done(((bf16[96,768]{1,0:T(8,128)(2,1)}), bf16[768,768]{1,0:T(8,128)(2,1)}) %all-gather.3.cloned.1.call-update) | async-done | bytes 1179664 | tf_op jit(solution)/shard_map/all_gather | solution.py:528
  109.7 4.9 %fusion.46 = (f32[768]{0:T(1024)S(1)}, bf16[1024,768]{1,0:T(8,128)(2,1)}) fusion(f32[1024,768]{1,0:T(8,128)} %get-tuple-element.113, f32[768]{0:T(1024)S(1)} %slice_reduce_fusion.1, bf16[1024,768]{1,0:T(8,128)(2,1)S(1)} %bitcast.98, bf16[768,768]{1,0:T(8,128)(2,1)} %all-gather.3.cloned.1.call-done), kind=kOutput, calls=%fused_computation.69 | convolution fusion | flops 1217395968 | bytes 7477248 | tf_op jit(solution)/shard_map/dot_general | solution.py:33
  114.7 3.3 %convolution_convert_fusion.1 = bf16[1024,768]{1,0:T(8,128)(2,1)S(1)} fusion(bf16[1024,768]{1,0:T(8,128)(2,1)} %copy-done.16, bf16[768,768]{1,0:T(8,128)(2,1)} %all-gather.3.cloned.1.call-done), kind=kOutput, calls=%fused_computation.23 | convolution fusion | flops 1208745984 | bytes 4325376 | tf_op jit(solution)/shard_map/dot_general | solution.py:37
  118.1 1.4 convolution_convert_fusion.2
  119.5 30.3 %shard_map.298 = (f32[256,768]{1,0:T(8,128)S(1)}, bf16[4,256,768]{2,1,0:T(8,128)(2,1)S(1)}, f32[256,768]{1,0:T(8,128)S(1)}, f32[8,768]{1,0:T(8,128)S(1)}) custom-call(bf16[4,256,768]{2,1,0:T(8,128)(2,1)S(1)} %bitcast.101, bf16[4,256,768]{2,1,0:T(8,128)(2,1)S(1)} %bitcast.100, f32[256,768]{1,0:T(8,128)S(1)} %copy-done.20, f32[256,768]{1,0:T(8,128)S(1)} %bitcast.91, ...), custom_call_target="tpu_custom_call" | custom-call | flops 20000000000 | bytes 4000000 | tf_op jit(solution)/shard_map/pallas_call | solution.py:616
  149.9 2.1 convolution_convert_fusion.4
  152.0 3.3 %fusion.49 = (f32[3,64]{1,0:T(4,128)S(1)}, bf16[1024,3,64]{0,2,1:T(8,128)(2,1)}) fusion(bf16[1024,3,64]{0,2,1:T(8,128)(2,1)S(1)} %bitcast.106, f32[3,1024,1024]{1,2,0:T(8,128)S(1)} %bitcast.103, f32[3,1024]{1,0:T(4,128)S(1)} %log_add_fusion), kind=kOutput, calls=%fused_computation.72 | convolution fusion | flops 412483392 | bytes 13382400 | tf_op jit(solution)/shard_map/while/body/eval_jaxpr/hqk,qhd->khd/dot_general | solution.py:477
  155.3 2.0 copy.51
  157.3 7.3 %fusion.53 = f32[3,1024,1024]{1,2,0:T(8,128)} fusion(bf16[1024,3,64]{0,2,1:T(8,128)(2,1)} %bitcast.107, bf16[1024,3,64]{0,2,1:T(8,128)(2,1)S(1)} %bitcast.105), kind=kOutput, calls=%fused_computation.74 | convolution fusion | flops 402653184 | bytes 13369344 | tf_op jit(solution)/shard_map/while/body/eval_jaxpr/qhd,khd->hqk/dot_general | solution.py:480
  164.7 19.7 %fusion.48 = (f32[3,64]{1,0:T(4,128)S(1)}, bf16[1024,3,64]{0,2,1:T(8,128)(2,1)}) fusion(bf16[1024,3,64]{0,2,1:T(8,128)(2,1)} %bitcast.113, f32[3,1024,1024]{1,2,0:T(8,128)} %fusion.53, f32[3,1024,1024]{1,2,0:T(8,128)} %copy-done.21, f32[3,1024]{1,0:T(4,128)S(1)} %log_add_fusion), kind=kOutput, calls=%fused_computation.71 | convolution fusion | flops 431361856 | bytes 25965312 | tf_op jit(solution)/shard_map/while/body/eval_jaxpr/hqk,khd->qhd/dot_general | solution.py:485
  184.5 19.5 %fusion.27 = bf16[3,64,1024]{2,1,0:T(8,128)(2,1)} fusion(bf16[1024,3,64]{0,2,1:T(8,128)(2,1)S(1)} %bitcast.111, f32[3,1024,1024]{1,2,0:T(8,128)} %fusion.53, f32[3,1024,1024]{1,2,0:T(8,128)} %copy-done.21, f32[3,1024]{1,0:T(4,128)S(1)} %log_add_fusion), kind=kOutput, calls=%fused_computation.32 | convolution fusion | flops 431165440 | bytes 25964544 | tf_op jit(solution)/shard_map/while/body/eval_jaxpr/hqk,qhd->khd/dot_general | solution.py:488
  204.1 2.0 copy.50
  206.1 2.0 copy.49
  208.1 1.2 shard_map.300
  209.3 2.0 pad_maximum_fusion.b_ref
  211.3 2.0 shard_map.299
  213.3 2.2 shard_map.302
  216.5 3.8 %convolution_convert_fusion = bf16[1024,768]{1,0:T(8,128)(2,1)} fusion(bf16[1024,576]{1,0:T(8,128)(2,1)S(1)} %pad_maximum_fusion.b_ref, bf16[768,768]{1,0:T(8,128)(2,1)} %bitcast.89), kind=kOutput, calls=%fused_computation.22 | convolution fusion | flops 906756096 | bytes 3735552 | tf_op jit(solution)/shard_map/dot_general | solution.py:37
  221.8 1.4 copy-done.13
  224.3 47.0 %shard_map.301 = (f32[256,768]{1,0:T(8,128)S(1)}, f32[96,768]{1,0:T(8,128)S(1)}, f32[8,768]{1,0:T(8,128)S(1)}) custom-call(bf16[4,256,768]{2,1,0:T(8,128)(2,1)S(1)} %bitcast.99, f32[256,768]{1,0:T(8,128)S(1)} %bitcast.94, f32[256,768]{1,0:T(8,128)S(1)} %copy-done.18, f32[8,768]{1,0:T(8,128)S(1)} %get-tuple-element.78.vec_ref, ...), custom_call_target="tpu_custom_call" | custom-call | flops 20000000000 | bytes 4000000 | tf_op jit(solution)/shard_map/pallas_call | solution.py:645
  274.4 1.6 convert_element_type.105
  276.1 27.2 %reduce-scatter.3.cloned.1.call-done = bf16[96,768]{1,0:T(8,128)(2,1)} async-done(((bf16[768,768]{1,0:T(8,128)(2,1)}), bf16[96,768]{1,0:T(8,128)(2,1)}) %reduce-scatter.3.cloned.1.call-update) | async-done | bytes 147472 | tf_op jit(solution)/shard_map/reduce_scatter | solution.py:613
  303.2 1.6 convert_element_type.104
  (123 shorter events, 23.3 us)
Async XLA Ops:
  7.2 78.6 %all-gather.5.cloned.1.call-start = ((), (), s32[]{:S(2)}) async-start(), calls=%async_computation.3 | async-start | bytes 1327104 | tf_op jit(solution)/shard_map/all_gather | solution.py:527
  7.9 101.7 %all-gather.3.cloned.1.call-start = ((), (), s32[]{:S(2)}) async-start(), calls=%async_computation.2 | async-start | bytes 1327104 | tf_op jit(solution)/shard_map/all_gather | solution.py:528
  8.7 265.7 %reduce-scatter.5.cloned.1.call-start = ((), (), s32[]{:S(2)}) async-start(), calls=%async_computation.5 | async-start | bytes 1327104 | tf_op jit(solution)/shard_map/reduce_scatter | solution.py:614
  13.5 1.1 copy-start.4
  49.8 1.2 copy-start
  49.8 1.7 copy-start.11
  49.8 9.2 %copy-start.3 = (bf16[8,96,768]{2,1,0:T(8,128)(2,1)}, bf16[8,96,768]{2,1,0:T(8,128)(2,1)S(1)}, u32[]{:S(2)}) copy-start(bf16[8,96,768]{2,1,0:T(8,128)(2,1)S(1)} %get-tuple-element.77) | copy-start | bytes 3538948
  51.6 1.9 copy-start.26
  51.6 1.9 copy-start.28
  51.6 4.0 %copy-start.22 = (bf16[1,1024,192]{1,2,0:T(8,128)(2,1)}, bf16[1,1024,192]{1,2,0:T(8,128)(2,1)S(1)}, u32[]{:S(2)}) copy-start(bf16[1,1024,192]{1,2,0:T(8,128)(2,1)S(1)} %get-tuple-element.94) | copy-start | bytes 1179652
  53.5 4.5 %copy-start.21 = (f32[3,1024,1024]{1,2,0:T(8,128)}, f32[3,1024,1024]{1,2,0:T(8,128)S(1)}, u32[]{:S(2)}) copy-start(f32[3,1024,1024]{1,2,0:T(8,128)S(1)} %get-tuple-element.110) | copy-start | bytes 37748740
  60.8 1.1 copy-start.7
  83.8 1.1 copy-start.9
  85.8 6.2 %copy-start.12 = (bf16[4,256,768]{2,1,0:T(8,128)(2,1)S(1)}, bf16[4,256,768]{2,1,0:T(8,128)(2,1)}, u32[]{:S(2)}) copy-start(bf16[4,256,768]{2,1,0:T(8,128)(2,1)} %copy-done.11) | copy-start | bytes 4718596
  90.8 1.2 copy-start.16
  114.6 3.4 %copy-start.14 = (bf16[1024,768]{1,0:T(8,128)(2,1)S(1)}, bf16[1024,768]{1,0:T(8,128)(2,1)}, u32[]{:S(2)}) copy-start(bf16[1024,768]{1,0:T(8,128)(2,1)} %get-tuple-element.91.b_ref) | copy-start | bytes 4718596
  114.6 3.4 %copy-start.29 = (bf16[768,768]{1,0:T(8,128)(2,1)S(1)}, bf16[768,768]{1,0:T(8,128)(2,1)}, u32[]{:S(2)}) copy-start(bf16[768,768]{1,0:T(8,128)(2,1)} %all-gather.5.cloned.1.call-done) | copy-start | bytes 3538948
  114.7 188.6 %reduce-scatter.3.cloned.1.call-start = ((), (), s32[]{:S(2)}) async-start(), calls=%async_computation.4 | async-start | bytes 1327104 | tf_op jit(solution)/shard_map/reduce_scatter | solution.py:613
  118.0 1.5 copy-start.5
  118.1 1.5 copy-start.20
  119.5 32.4 %slice-start = ((s8[12582912]{0:T(1024)(128)(4,1)}), s8[4194304]{0:T(1024)(128)(4,1)S(1)}, s32[]{:S(2)}) async-start(s8[12582912]{0:T(1024)(128)(4,1)} %bitcast.102), calls=%async_computation.6 | async-start | bytes 8388608
  119.5 32.4 %slice-start.1 = ((s8[12582912]{0:T(1024)(128)(4,1)}), s8[4194304]{0:T(1024)(128)(4,1)S(1)}, s32[]{:S(2)}) async-start(s8[12582912]{0:T(1024)(128)(4,1)} %bitcast.102), calls=%async_computation.7 | async-start | bytes 8388608
  119.5 32.4 %slice-start.2 = ((s8[12582912]{0:T(1024)(128)(4,1)}), s8[4194304]{0:T(1024)(128)(4,1)S(1)}, s32[]{:S(2)}) async-start(s8[12582912]{0:T(1024)(128)(4,1)} %bitcast.102), calls=%async_computation.8 | async-start | bytes 8388608
  149.8 5.4 %copy-start.17 = (f32[256,768]{1,0:T(8,128)}, f32[256,768]{1,0:T(8,128)S(1)}, u32[]{:S(2)}) copy-start(f32[256,768]{1,0:T(8,128)S(1)} %get-tuple-element.83.mixed_grad_ref) | copy-start | bytes 2359300
  151.9 3.3 %copy-start.24 = (bf16[1024,192]{0,1:T(8,128)(2,1)}, bf16[1024,192]{0,1:T(8,128)(2,1)S(1)}, u32[]{:S(2)}) copy-start(bf16[1024,192]{0,1:T(8,128)(2,1)S(1)} %convolution_convert_fusion.4) | copy-start | bytes 1179652
  152.0 5.4 %copy-start.23 = (bf16[1,1024,192]{1,2,0:T(8,128)(2,1)S(1)}, bf16[1,1024,192]{1,2,0:T(8,128)(2,1)}, u32[]{:S(2)}) copy-start(bf16[1,1024,192]{1,2,0:T(8,128)(2,1)} %copy-done.22) | copy-start | bytes 1179652
  164.7 19.9 %copy-start.27 = (bf16[1,1024,192]{1,2,0:T(8,128)(2,1)S(1)}, bf16[1,1024,192]{1,2,0:T(8,128)(2,1)}, u32[]{:S(2)}) copy-start(bf16[1,1024,192]{1,2,0:T(8,128)(2,1)} %copy-done.26) | copy-start | bytes 1179652
  208.1 3.2 %copy-start.1 = (bf16[4,256,768]{2,1,0:T(8,128)(2,1)S(1)}, bf16[4,256,768]{2,1,0:T(8,128)(2,1)}, u32[]{:S(2)}) copy-start(bf16[4,256,768]{2,1,0:T(8,128)(2,1)} %copy-done) | copy-start | bytes 4718596
  209.3 4.0 %copy-start.10 = (bf16[4,256,768]{2,1,0:T(8,128)(2,1)S(1)}, bf16[4,256,768]{2,1,0:T(8,128)(2,1)}, u32[]{:S(2)}) copy-start(bf16[4,256,768]{2,1,0:T(8,128)(2,1)} %copy-done.9) | copy-start | bytes 4718596
  209.3 4.0 %copy-start.15 = (bf16[1024,768]{1,0:T(8,128)(2,1)S(1)}, bf16[1024,768]{1,0:T(8,128)(2,1)}, u32[]{:S(2)}) copy-start(bf16[1024,768]{1,0:T(8,128)(2,1)} %get-tuple-element.91.b_ref) | copy-start | bytes 4718596
  220.6 1.1 copy-start.8
  221.8 1.4 copy-start.13
  (5 other events, 4.9 us)
Sparse Core Ops, SparseCore 0:
  10.2 57.0 all-gather.4
  69.5 40.1 all-gather.2
  114.8 67.4 reduce-scatter.4
  220.5 82.6 reduce-scatter.2

commit v2 on v1

--- a/solution.py
+++ b/solution.py
@@ -56,14 +56,12 @@
     for peer in tensor_peers:
         pl.semaphore_signal(barrier, inc=1, device_id=(d, peer), device_id_type=MESH)
 
-    def signal(k, carry):
+    def signal(k):
         pl.semaphore_signal(
             barrier, inc=1, device_id=(lax.rem(d + k, dp), t), device_id_type=MESH
         )
-        return carry
-
-    if dp > 1:
-        lax.fori_loop(1, dp, signal, 0)
+
+    each_peer(dp, signal)
     pl.semaphore_wait(barrier, len(tensor_peers) + dp - 1)
 
 
@@ -221,25 +219,135 @@
     lax.fori_loop(1, dp, step, 0)
 
 
+def pair_copy(src, dst, sem_pair, index, peer):
+    t = lax.axis_index("tensor")
+    return pltpu.make_async_remote_copy(
+        src_ref=src,
+        dst_ref=dst,
+        send_sem=sem_pair[0].at[index],
+        recv_sem=sem_pair[1].at[index],
+        device_id=(peer, t),
+        device_id_type=MESH,
+    )
+
+
+class WeightGather:
+    def __init__(self, dp, own, out, slow_sems, fast_sems):
+        self.dp, self.half = dp, dp // 2
+        self.own, self.out = own, out
+        self.slow_sems, self.fast_sems = slow_sems, fast_sems
+        self.d = lax.axis_index("dp")
+        self.f = lax.rem(self.d, 2)
+        self.partner = self.d + 1 - 2 * self.f
+
+    def slow(self, k):
+        peer = lax.rem(self.d + 2 * k, self.dp)
+        return pair_copy(self.own, self.out.at[self.d], self.slow_sems, k, peer)
+
+    def fast(self, k):
+        if isinstance(k, int) and k == 0:
+            return pair_copy(self.own, self.out.at[self.d], self.fast_sems, 0, self.partner)
+        source = lax.rem(self.d + self.dp - 2 * k, self.dp)
+        ref = self.out.at[source]
+        return pair_copy(ref, ref, self.fast_sems, k, self.partner)
+
+    def start(self):
+        each_peer(self.half, lambda k: self.slow(k).start())
+        self.fast(0).start()
+
+    def forward(self):
+        def step(k):
+            self.slow(k).wait_recv()
+            self.fast(k).start()
+
+        each_peer(self.half, step)
+
+    def finish(self):
+        self.fast(0).wait()
+        each_peer(self.half, lambda k: self.fast(k).wait())
+        each_peer(self.half, lambda k: self.slow(k).wait_send())
+
+
+class WeightScatter:
+    def __init__(self, dp, part, near, total, far, slow_sems, fast_sems):
+        self.dp, self.half = dp, dp // 2
+        self.part, self.near, self.total, self.far = part, near, total, far
+        self.slow_sems, self.fast_sems = slow_sems, fast_sems
+        self.d = lax.axis_index("dp")
+        self.f = lax.rem(self.d, 2)
+        self.partner = self.d + 1 - 2 * self.f
+
+    def fast(self, k):
+        target = lax.rem(self.partner + 2 * k, self.dp)
+        return pair_copy(
+            self.part.at[target], self.near.at[k], self.fast_sems, k, self.partner
+        )
+
+    def slow(self, k):
+        peer = lax.rem(self.d + 2 * k, self.dp)
+        return pair_copy(self.total.at[k], self.far.at[k], self.slow_sems, k, peer)
+
+    def start(self):
+        each_peer(self.half, lambda k: self.fast(k).start())
+        self.fast(0).start()
+
+    def middle(self):
+        def step(k):
+            self.fast(k).wait_recv()
+            target = lax.rem(self.d + 2 * k, self.dp)
+            self.total[k] = (self.part[target].astype(F32) + self.near[k].astype(F32)).astype(
+                BF16
+            )
+            self.slow(k).start()
+
+        each_peer(self.half, step)
+
+    def result(self):
+        self.fast(0).wait_recv()
+        acc = self.part[self.d].astype(F32) + self.near[0].astype(F32)
+        for k in range(1, self.half):
+            self.slow(k).wait_recv()
+            acc = acc + self.far[k].astype(F32)
+        return acc
+
+    def finish(self):
+        self.fast(0).wait_send()
+        each_peer(self.half, lambda k: self.fast(k).wait_send())
+        each_peer(self.half, lambda k: self.slow(k).wait_send())
+
+
+def sem_pairs(dp):
+    return [pltpu.SemaphoreType.DMA((dp // 2,)) for _ in range(4)]
+
+
+def weight_scratch(dp, shard, width):
+    return [pltpu.VMEM((dp // 2, shard, width), BF16) for _ in range(3)] + sem_pairs(dp)
+
+
 def first_kernel(
-    dp, x_ref, cot_ref, small_ref, pack_ref,
-    gathered_ref, vec_ref, low_ref, cot_all_ref,
-    small_buf, s_send, s_recv, w_send, w_recv, own_sem, l_send, l_recv, c_send, c_recv,
+    dp, x_ref, cot_ref, small_ref, pack_ref, inner_ref,
+    gathered_ref, inner_all_ref, vec_ref, low_ref, cot_all_ref,
+    small_buf, s_send, s_recv, own_sem, l_send, l_recv, c_send, c_recv,
+    p0, p1, p2, p3, i0, i1, i2, i3,
 ):
     d, t, sib, opp, diag = places()
-    own = pltpu.make_async_copy(pack_ref, gathered_ref.at[d], own_sem)
-    own.start()
+    owns = [
+        pltpu.make_async_copy(pack_ref, gathered_ref.at[d], own_sem.at[0]),
+        pltpu.make_async_copy(inner_ref, inner_all_ref.at[d], own_sem.at[1]),
+    ]
+    for own in owns:
+        own.start()
     small_buf[d] = small_ref[...]
     greet(dp, (sib, opp))
 
     def small_copy(k):
         return dp_copy(dp, k, small_buf.at[d], small_buf.at[d], s_send, s_recv)
 
-    def pack_copy(k):
-        return dp_copy(dp, k, pack_ref, gathered_ref.at[d], w_send, w_recv)
-
+    pack = WeightGather(dp, pack_ref, gathered_ref, (p0, p1), (p2, p3))
+    inner = WeightGather(dp, inner_ref, inner_all_ref, (i0, i1), (i2, i3))
     each_peer(dp, lambda k: small_copy(k).start())
-    each_peer(dp, lambda k: pack_copy(k).start())
+    pack.start()
+    inner.start()
     low = Gather(low_ref, l_send, l_recv)
     cot = Gather(cot_all_ref, c_send, c_recv)
     each_peer(dp, lambda k: small_copy(k).wait_recv())
@@ -252,27 +360,36 @@
     for c in range(cot.chunks):
         cot_all_ref[t, rows_of(c), :] = cot_ref[rows_of(c), :].astype(BF16)
         cot.start(c)
+    pack.forward()
     for c in range(low.chunks):
         low.forward(c)
+    inner.forward()
     for c in range(cot.chunks):
         cot.forward(c)
     low.finish()
     cot.finish()
     each_peer(dp, lambda k: small_copy(k).wait_send())
-    each_peer(dp, lambda k: pack_copy(k).wait())
-    own.wait()
+    pack.finish()
+    inner.finish()
+    for own in owns:
+        own.wait()
 
 
 def second_kernel(
-    part_ref, x_ref, vec_ref,
-    mixed_ref, low_ref,
+    dp, part_ref, x_ref, vec_ref, outer_ref,
+    mixed_ref, low_ref, outer_all_ref,
     near, total, far, r_send, r_recv, l_send, l_recv,
+    own_sem, o0, o1, o2, o3,
 ):
     d, t, sib, opp, diag = places()
-    greet(1, (sib, opp))
+    own = pltpu.make_async_copy(outer_ref, outer_all_ref.at[d], own_sem)
+    own.start()
+    greet(dp, (sib, opp))
     scat = Scatter(part_ref, near, total, far, r_send, r_recv)
     low = Gather(low_ref, l_send, l_recv)
+    outer = WeightGather(dp, outer_ref, outer_all_ref, (o0, o1), (o2, o3))
     scat.start()
+    outer.start()
     for c in range(scat.chunks):
         scat.middle(c)
     bias, gain, shift = vec_ref[2:3, :], vec_ref[3:4, :], vec_ref[4:5, :]
@@ -282,25 +399,34 @@
         normed, _ = normed_rows(mixed)
         low_ref[t, rows_of(c), :] = (normed * gain + shift).astype(BF16)
         low.start(c)
+    outer.forward()
     for c in range(low.chunks):
         low.forward(c)
     low.finish()
     scat.finish()
+    outer.finish()
+    own.wait()
 
 
 def third_kernel(
-    npart_ref, fpart_ref, mixed_ref, cot_ref, vec_ref,
-    grad_ref, all_ref, out_ref, sums_ref,
+    dp, npart_ref, fpart_ref, mixed_ref, cot_ref, vec_ref, wo_ref, wi_ref,
+    grad_ref, all_ref, out_ref, sums_ref, wo_out_ref, wi_out_ref,
     n_near, n_total, n_far, n_send, n_recv,
     f_near, f_total, f_far, f_send, f_recv,
     g_send, g_recv,
+    o_near, o_total, o_far, o0, o1, o2, o3,
+    i_near, i_total, i_far, i0, i1, i2, i3,
 ):
     d, t, sib, opp, diag = places()
-    greet(1, (sib, opp))
+    greet(dp, (sib, opp))
+    outer = WeightScatter(dp, wo_ref, o_near, o_total, o_far, (o0, o1), (o2, o3))
+    inner = WeightScatter(dp, wi_ref, i_near, i_total, i_far, (i0, i1), (i2, i3))
     first = Scatter(npart_ref, n_near, n_total, n_far, n_send, n_recv)
     feed = Scatter(fpart_ref, f_near, f_total, f_far, f_send, f_recv)
     gather = Gather(all_ref, g_send, g_recv)
     first.start()
+    outer.start()
+    inner.start()
     for c in range(first.chunks):
         first.middle(c)
     feed.start()
@@ -320,35 +446,38 @@
     sums_ref[...] = jnp.concatenate([zero, zero] + sums + [zero, zero], axis=0)
     for c in range(feed.chunks):
         feed.middle(c)
+    outer.middle()
     for c in range(gather.chunks):
         gather.forward(c)
+    inner.middle()
     bias = vec_ref[5:6, :]
     for c in range(feed.chunks):
         out_ref[rows_of(c), :] = mixed_ref[rows_of(c), :] + feed.result(c) + bias
     gather.finish()
+    wo_out_ref[...] = outer.result()
+    wi_out_ref[...] = inner.result()
     first.finish()
     feed.finish()
+    outer.finish()
+    inner.finish()
 
 
 def fourth_kernel(
     dp, part_ref, x_ref, mixed_grad_ref, vec_ref, sums_ref, wgrad_ref,
     input_grad_ref, wout_ref, vout_ref,
     near, total, far, r_send, r_recv,
-    landed, w_send, w_recv, group, t_send, t_recv, whole, v_send, v_recv,
+    w_near, w_total, w_far, w0, w1, w2, w3, group, t_send, t_recv, whole, v_send, v_recv,
 ):
     d, t, sib, opp, diag = places()
     greet(dp, (sib, opp, diag))
     scat = Scatter(part_ref, near, total, far, r_send, r_recv)
     scat.start()
 
-    def weight_copy(k):
-        return dp_copy(
-            dp, k, wgrad_ref.at[lax.rem(d + k, dp)], landed.at[d], w_send, w_recv
-        )
-
-    each_peer(dp, lambda k: weight_copy(k).start())
+    weights = WeightScatter(dp, wgrad_ref, w_near, w_total, w_far, (w0, w1), (w2, w3))
+    weights.start()
     for c in range(scat.chunks):
         scat.middle(c)
+    weights.middle()
     gain = vec_ref[0:1, :]
     sums = [jnp.zeros_like(gain) for _ in range(2)]
     for c in range(scat.chunks):
@@ -386,15 +515,11 @@
         return dp_copy(dp, k, whole.at[d], whole.at[d], v_send, v_recv)
 
     each_peer(dp, lambda k: vector_copy(k).start())
-    landed[d] = wgrad_ref[d]
-    each_peer(dp, lambda k: weight_copy(k).wait())
-    acc = landed[0].astype(F32)
-    for k in range(1, dp):
-        acc = acc + landed[k].astype(F32)
-    wout_ref[...] = acc
+    wout_ref[...] = weights.result()
     each_peer(dp, lambda k: vector_copy(k).wait())
     vout_ref[...] = jnp.sum(whole[...], axis=0)
     scat.finish()
+    weights.finish()
 
 
 VM = pl.BlockSpec(memory_space=pltpu.VMEM)
@@ -462,37 +587,73 @@
     return (context.reshape(queries.shape).astype(jnp.bfloat16), log_total)
 
 
-def attend_back(operands):
-    queries, key_rows, values, context_grad, log_total = operands
-    score_scale = 1.0 / math.sqrt(HD)
-    query_heads = split_heads(queries)
-    key_heads = split_heads(key_rows)
-    grad_heads = split_heads(context_grad)
-    scores = (
-        jnp.einsum("qhd,khd->hqk", query_heads, key_heads, preferred_element_type=jnp.float32)
-        * score_scale
-    )
-    prob_full = jnp.exp(scores - log_total)
-    prob_low = prob_full.astype(jnp.bfloat16)
-    value_grad = jnp.einsum(
-        "hqk,qhd->khd", prob_low, grad_heads, preferred_element_type=jnp.float32
-    )
-    prob_grad = jnp.einsum(
-        "qhd,khd->hqk", grad_heads, split_heads(values), preferred_element_type=jnp.float32
-    )
-    row_dot = jnp.sum(prob_full * prob_grad, axis=-1, keepdims=True)
-    score_grad = (prob_full * (prob_grad - row_dot) * score_scale).astype(jnp.bfloat16)
-    query_grad = jnp.einsum(
-        "hqk,khd->qhd", score_grad, key_heads, preferred_element_type=jnp.float32
-    )
-    key_low = jnp.einsum(
-        "hqk,qhd->khd", score_grad, query_heads, preferred_element_type=jnp.float32
-    ).astype(jnp.bfloat16)
-    return (
-        query_grad.reshape(queries.shape),
-        key_low.reshape(queries.shape),
-        value_grad.reshape(queries.shape),
-    )
+def attend_back_kernel(heads, qkv_ref, grad_ref, log_ref, out_ref, sums_ref, queries_t, keys, vals):
+    scale = 1.0 / math.sqrt(HD)
+    width = heads * HD
+    frames = qkv_ref.shape[0]
+    tile = 256
+    for h in range(heads):
+        lanes = slice(h * HD, (h + 1) * HD)
+        key = qkv_ref[:, width + h * HD : width + (h + 1) * HD]
+        value = qkv_ref[:, 2 * width + h * HD : 2 * width + (h + 1) * HD]
+        key_t = key.astype(F32).T.astype(BF16)
+        keys[...] = jnp.zeros_like(keys)
+        vals[...] = jnp.zeros_like(vals)
+
+        def step(i, carry, lanes=lanes, key=key, value=value, key_t=key_t, h=h):
+            start = pl.multiple_of(i * tile, tile)
+            at = pl.ds(start, tile)
+            query = qkv_ref[at, lanes]
+            grad = grad_ref[at, lanes]
+            scores = matmul_nt(key, query) * scale
+            prob = jnp.exp(scores - log_ref[h : h + 1, at])
+            vals[...] += matmul(prob.astype(BF16), grad)
+            prob_grad = matmul_nt(value, grad)
+            row_dot = jnp.sum(prob * prob_grad, axis=0, keepdims=True)
+            score_grad = (prob * (prob_grad - row_dot) * scale).astype(BF16)
+            keys[...] += matmul(score_grad, query)
+            queries_t[lanes, at] = matmul(key_t, score_grad)
+            return carry
+
+        lax.fori_loop(0, frames // tile, step, 0)
+        value_grad = vals[...]
+        out_ref[:, width + h * HD : width + (h + 1) * HD] = keys[...].astype(BF16)
+        out_ref[:, 2 * width + h * HD : 2 * width + (h + 1) * HD] = value_grad.astype(BF16)
+        query_grad = queries_t[lanes, :].T
+        out_ref[:, lanes] = query_grad.astype(BF16)
+        sums_ref[0:1, lanes] = jnp.sum(query_grad, axis=0, keepdims=True)
+        sums_ref[1:2, lanes] = jnp.sum(value_grad, axis=0, keepdims=True)
+
+
+def attend_back(qkv, context_grad, log_total):
+    clips, frames, wide = qkv.shape
+    width = context_grad.shape[2]
+    heads = width // HD
+
+    def spec(*shape):
+        return pl.BlockSpec((None,) + shape, lambda c: (c, 0, 0))
+
+    return pl.pallas_call(
+        functools.partial(attend_back_kernel, heads),
+        grid=(clips,),
+        out_shape=(
+            jax.ShapeDtypeStruct((clips, frames, wide), BF16),
+            jax.ShapeDtypeStruct((clips, 2, width), F32),
+        ),
+        in_specs=[spec(frames, wide), spec(frames, width), spec(heads, frames)],
+        out_specs=(spec(frames, wide), spec(2, width)),
+        scratch_shapes=[
+            pltpu.VMEM((width, frames), F32),
+            pltpu.VMEM((frames, HD), F32),
+            pltpu.VMEM((frames, HD), F32),
+        ],
+        cost_estimate=pl.CostEstimate(
+            flops=10 * clips * heads * frames * frames * HD,
+            bytes_accessed=6_000_000,
+            transcendentals=clips * heads * frames * frames,
+        ),
+        compiler_params=pltpu.CompilerParams(vmem_limit_bytes=36 * 1024 * 1024),
+    )(qkv, context_grad, log_total)
 
 
 def on_device(
@@ -524,9 +685,6 @@
     shard = query_weight.shape[0]
     hidden_units = inner_weight.shape[1]
 
-    inner_full = lax.all_gather(inner_weight, "dp", axis=0, tiled=True)
-    outer_full = lax.all_gather(outer_weight, "dp", axis=0, tiled=True)
-
     def placed_bias(bias):
         full = jnp.zeros((HD, bias.shape[1]), F32)
         full = lax.dynamic_update_slice(full, bias.astype(F32), (d * bias.shape[0], 0))
@@ -560,23 +718,24 @@
             .reshape(block)
         )
 
-    gathered_pack, vec, low_one, cot_all = comm_call(
+    gathered_pack, inner_all, vec, low_one, cot_all = comm_call(
         functools.partial(first_kernel, dp),
         1,
-        [VM, VM, VM, ANY],
-        [((dp,) + pack.shape, BF16), ((VROWS, feats), F32), (block, BF16), (block, BF16)],
-        [ANY, VM, VM, VM],
+        [VM, VM, VM, ANY, ANY],
+        [((dp,) + pack.shape, BF16), ((dp,) + inner_weight.shape, BF16), ((VROWS, feats), F32), (block, BF16), (block, BF16)],
+        [ANY, ANY, VM, VM, VM],
         [
             pltpu.VMEM((dp, VROWS, feats), F32),
             pltpu.SemaphoreType.DMA((dp,)),
             pltpu.SemaphoreType.DMA((dp,)),
-            pltpu.SemaphoreType.DMA((dp,)),
-            pltpu.SemaphoreType.DMA((dp,)),
-            pltpu.SemaphoreType.DMA,
+            pltpu.SemaphoreType.DMA((2,)),
         ]
         + gather_scratch(rows)
-        + gather_scratch(rows),
-    )(x, cot, small, pack)
+        + gather_scratch(rows)
+        + sem_pairs(dp)
+        + sem_pairs(dp),
+    )(x, cot, small, pack, inner_weight)
+    inner_full = inner_all.reshape(feats, hidden_units)
     flat_one = to_tokens(low_one)
     cot_tokens = to_tokens(cot_all)
     attn_weights = gathered_pack.reshape(feats, 4 * width)
@@ -591,14 +750,18 @@
     flat_context = context.reshape(clips * frames, width)
     attn_part = to_blocks(matmul_nt(flat_context, output_full))
 
-    mixed, low_two = comm_call(
-        second_kernel,
+    mixed, low_two, outer_all = comm_call(
+        functools.partial(second_kernel, dp),
         2,
-        [VM, VM, VM],
-        [((rows, feats), F32), (block, BF16)],
-        [VM, VM],
-        scatter_scratch(rows, feats) + gather_scratch(rows),
-    )(attn_part, x, vec)
+        [VM, VM, VM, ANY],
+        [((rows, feats), F32), (block, BF16), ((dp,) + outer_weight.shape, BF16)],
+        [VM, VM, ANY],
+        scatter_scratch(rows, feats)
+        + gather_scratch(rows)
+        + [pltpu.SemaphoreType.DMA]
+        + sem_pairs(dp),
+    )(attn_part, x, vec, outer_weight)
+    outer_full = outer_all.reshape(feats, hidden_units)
     flat_two = to_tokens(low_two)
     preact = matmul(flat_two, inner_full) + vec[7, :hidden_units]
     hidden = gelu_value(preact).astype(BF16)
@@ -610,33 +773,44 @@
 
     outer_part = token_product(cot_tokens, hidden)
     inner_part = token_product(flat_two, preact_low)
-    inner_weight_grad = lax.psum_scatter(inner_part, "dp", scatter_dimension=0, tiled=True)
-    outer_weight_grad = lax.psum_scatter(outer_part, "dp", scatter_dimension=0, tiled=True)
-
-    mixed_grad, mixed_all, layer_output, sums = comm_call(
-        third_kernel,
+    by_shard = (dp, shard, hidden_units)
+
+    (
+        mixed_grad, mixed_all, layer_output, sums, outer_weight_grad, inner_weight_grad,
+    ) = comm_call(
+        functools.partial(third_kernel, dp),
         3,
-        [VM] * 5,
-        [((rows, feats), F32), (block, BF16), ((rows, feats), F32), ((VROWS, feats), F32)],
-        [VM] * 4,
-        scatter_scratch(rows, feats) + scatter_scratch(rows, feats) + gather_scratch(rows),
-    )(norm_two_part, feed_part, mixed, cot, vec)
+        [VM] * 7,
+        [
+            ((rows, feats), F32),
+            (block, BF16),
+            ((rows, feats), F32),
+            ((VROWS, feats), F32),
+            ((shard, hidden_units), F32),
+            ((shard, hidden_units), F32),
+        ],
+        [VM] * 6,
+        scatter_scratch(rows, feats)
+        + scatter_scratch(rows, feats)
+        + gather_scratch(rows)
+        + weight_scratch(dp, shard, hidden_units)
+        + weight_scratch(dp, shard, hidden_units),
+    )(
+        norm_two_part, feed_part, mixed, cot, vec,
+        outer_part.reshape(by_shard), inner_part.reshape(by_shard),
+    )
     mixed_tokens = to_tokens(mixed_all)
     output_part = token_product(mixed_tokens, flat_context)
     context_grad = matmul(mixed_tokens, output_full).astype(BF16).reshape(clips, frames, width)
-    query_grad, key_low, value_grad = lax.map(
-        attend_back, (clip_queries, clip_keys, clip_values, context_grad, log_total)
-    )
-    query_grad = query_grad.reshape(clips * frames, width)
-    key_low = key_low.reshape(clips * frames, width)
-    value_grad = value_grad.reshape(clips * frames, width)
-    low_grads = jnp.concatenate(
-        [query_grad.astype(BF16), key_low, value_grad.astype(BF16)], axis=1
-    )
+    low_grads, head_sums = attend_back(
+        clip_qkv, context_grad, log_total.reshape(clips, width // HD, frames)
+    )
+    low_grads = low_grads.reshape(clips * frames, 3 * width)
+    head_sums = jnp.sum(head_sums, axis=0)
     norm_one_part = to_blocks(matmul_nt(low_grads, qkv_full))
     attn_wpart = jnp.concatenate([token_product(flat_one, low_grads), output_part], axis=1)
     bias_row = jnp.concatenate(
-        [jnp.sum(query_grad, axis=0), none, jnp.sum(value_grad, axis=0), none]
+        [head_sums[0], none, head_sums[1], none]
     )
     sums = sums + jnp.concatenate(
         [jnp.zeros((VROWS - 2, feats), F32), bias_row[None], inner_bias_sum[None]], axis=0
@@ -649,10 +823,8 @@
         [((rows, feats), F32), ((shard, 4 * width), F32), ((VROWS, feats), F32)],
         [VM] * 3,
         scatter_scratch(rows, feats)
+        + weight_scratch(dp, shard, 4 * width)
         + [
-            pltpu.VMEM((dp, shard, 4 * width), BF16),
-            pltpu.SemaphoreType.DMA((dp,)),
-            pltpu.SemaphoreType.DMA((dp,)),
             pltpu.VMEM((4, VROWS, feats), F32),
             pltpu.SemaphoreType.DMA((3,)),
             pltpu.SemaphoreType.DMA((3,)),
@@ -683,9 +855,9 @@
         mine[2],
         mine[3],
         mine[4],
-        inner_weight_grad.astype(F32),
+        inner_weight_grad,
         bias_share(vector_sums[7, :hidden_units], inner_bias),
-        outer_weight_grad.astype(F32),
+        outer_weight_grad,
         mine[5],
     )
 

time: 314 us -> 211 us (0.67)
  matrix products: 77.4 us -> 19.1 us
  waiting for transfers between devices: 43.4 us -> 0 us
  Pallas kernels: 141 us -> 165 us
  between operations: 14.3 us -> 1.15 us
  local copies, waits for them, and re-layouts: 26.4 us -> 20.6 us
  other arithmetic: 10.1 us -> 4.84 us
    dot_general x4 -> x0, matrix products: 49.8 us -> none  [the longest x1 19.7 us: attend_back(): jnp.einsum('hqk,khd->qhd', score_grad, key_heads, preferred_element_type=...]
    pallas_call x3 -> x4, Pallas kernels: 86.1 us -> 130 us  [the longest x1 44.6 us: on_device(): comm_call(functools.partial(first_kernel, dp), 1, [VM, VM, VM, ANY, ANY],...]
    reduce_scatter x2 -> x0, waiting for transfers between devices: 27.2 us -> none  [the longest x1 27.2 us: on_device(): lax.psum_scatter(inner_part, 'dp', scatter_dimension=0, tiled=True)]
    pallas_call x1, Pallas kernels: 47 us -> 27.7 us  [on_device(): comm_call(functools.partial(fourth_kernel, dp), 4, [VM] * 6, [((rows, fea...]
    all_gather x2 -> x0, waiting for transfers between devices: 14.9 us -> none  [the longest x1 14.9 us: on_device(): outer_full = lax.all_gather(outer_weight, 'dp', axis=0, tiled=True)]
    dot_general x4, matrix products: 13.1 us -> 8.79 us  [matmul(): return jnp.dot(left, right, preferred_element_type=F32)]
    unnamed x69 -> x55, local copies, waits for them, and re-layouts: 15.2 us -> 11 us
    dot_general x4, matrix products: 10.3 us -> 6.23 us  [matmul_nt(): lax.dot_general(left, right, (((1,), (1,)), ((), ())), preferred_element_...]
  transfers between devices with their start and end apart: 4 -> 0, of which waited for: 2 -> 0; matrix products, arithmetic and copies ran while one was open for 30% -> 0% of each run, Pallas kernels for 45% -> 0%
where the time goes in v2:
time: 211 us
  Pallas kernels  165 us (78%)
  local copies, waits for them, and re-layouts  20.6 us (10%)
  matrix products  19.1 us (9%)
  other arithmetic  4.84 us (2%)
    pallas_call x1, Pallas kernels, on_device(): comm_call(functools.partial(first_kernel, dp), 1, [VM, VM, VM, ANY, ANY],...  44.6 us
    pallas_call x1, Pallas kernels, on_device(): comm_call(functools.partial(third_kernel, dp), 3, [VM] * 7, [((rows, feat...  40.4 us
    pallas_call x1, Pallas kernels, on_device(): comm_call(functools.partial(second_kernel, dp), 2, [VM, VM, VM, ANY], [((...  27.9 us
    pallas_call x1, Pallas kernels, on_device(): comm_call(functools.partial(fourth_kernel, dp), 4, [VM] * 6, [((rows, fea...  27.7 us
    pallas_call x1, Pallas kernels, attend_back(): pl.pallas_call(functools.partial(attend_back_kernel, heads), grid=(clips,...  17 us
    unnamed x55, local copies, waits for them, and re-layouts  11 us
    dot_general x4, matrix products, matmul(): return jnp.dot(left, right, preferred_element_type=F32)  8.79 us
    pallas_call x4, Pallas kernels, token_product(): pl.pallas_call(token_kernel, grid=(m // tile,), out_shape=jax.ShapeDtypeS...  7.26 us

profile of v2, /device:TPU:0, one launch (start us, length us, event | category | flops | bytes accessed | tf_op | source)
XLA Modules:
  0.0 210.6 jit_solution(4728849699396967278)
XLA Ops:
  4.5 1.0 pad_maximum_fusion.1.pack_ref
  5.5 1.1 copy-done.8
  6.6 1.1 copy-done.10
  7.8 0.9 copy-done.13
  8.7 44.6 %shard_map.296 = (bf16[8,96,768]{2,1,0:T(8,128)(2,1)S(1)}, bf16[8,96,768]{2,1,0:T(8,128)(2,1)S(1)}, f32[8,768]{1,0:T(8,128)S(1)}, bf16[4,256,768]{2,1,0:T(8,128)(2,1)S(1)}, bf16[4,256,768]{2,1,0:T(8,128)(2,1)S(1)}) custom-call(f32[256,768]{1,0:T(8,128)S(1)} %bitcast.90, f32[256,768]{1,0:T(8,128)S(1)} %bitcast.88, f32[8,768]{1,0:T(8,128)S(1)} %pad_maximum_fusion.2.small_ref, ...), custom_call_target="tpu_custom_call" | custom-call | flops 20000000000 | bytes 4000000 | tf_op jit(solution)/shard_map/pallas_call | solution.py:721
  53.4 1.4 fusion.5.qkv_ref
  55.3 1.2 fusion.17
  56.6 0.9 copy.45
  57.5 1.2 copy.46
  58.7 1.2 copy.47
  60.0 1.9 multiply_reduce_fusion
  61.8 2.1 exponential_reduce_fusion
  63.9 2.2 %fusion.6 = bf16[3,64,1024]{2,1,0:T(8,128)(2,1)S(1)} fusion(bf16[1024,3,64]{0,2,1:T(8,128)(2,1)S(1)} %bitcast.110, f32[3,1024,1024]{1,2,0:T(8,128)S(1)} %get-tuple-element.93, f32[3,1024]{1,0:T(4,128)S(1)} %log_add_fusion), kind=kOutput, calls=%fused_computation.18 | convolution fusion | flops 412286976 | bytes 13381632 | tf_op jit(solution)/shard_map/while/body/eval_jaxpr/hqk,khd->qhd/dot_general | solution.py:584
  66.2 0.8 convolution_convert_fusion.3
  67.5 27.9 %shard_map.297 = (f32[256,768]{1,0:T(8,128)S(1)}, bf16[4,256,768]{2,1,0:T(8,128)(2,1)S(1)}, bf16[8,96,768]{2,1,0:T(8,128)(2,1)S(1)}) custom-call(bf16[4,256,768]{2,1,0:T(8,128)(2,1)S(1)} %bitcast.76, f32[256,768]{1,0:T(8,128)S(1)} %bitcast.91, f32[8,768]{1,0:T(8,128)S(1)} %get-tuple-element.57.vec_ref, bf16[96,768]{1,0:T(8,128)(2,1)S(1)} %copy-done.14), custom_call_target="tpu_custom_call" | custom-call | flops 20000000000 | bytes 4000000 | tf_op jit(solution)/shard_map/pallas_call | solution.py:753
  95.4 3.9 %multiply_convert_fusion = (bf16[1024,768]{1,0:T(8,128)(2,1)S(1)}, f32[1024,768]{1,0:T(8,128)S(1)}) fusion(f32[768]{0:T(1024)S(1)} %slice_reduce_fusion.1, bf16[1024,768]{1,0:T(8,128)(2,1)S(1)} %bitcast.96, bf16[768,768]{1,0:T(8,128)(2,1)S(1)} %bitcast.100), kind=kOutput, calls=%fused_computation.9 | convolution fusion | flops 1212678144 | bytes 7474176 | tf_op jit(solution)/shard_map/dot_general | solution.py:33
  99.2 2.8 %fusion.16 = (f32[768]{0:T(1024)S(1)}, bf16[1024,768]{1,0:T(8,128)(2,1)S(1)}) fusion(f32[1024,768]{1,0:T(8,128)S(1)} %get-tuple-element.96, f32[768]{0:T(1024)S(1)} %slice_reduce_fusion.1, bf16[1024,768]{1,0:T(8,128)(2,1)S(1)} %bitcast.93, bf16[768,768]{1,0:T(8,128)(2,1)S(1)} %bitcast.102), kind=kOutput, calls=%fused_computation.52 | convolution fusion | flops 1217395968 | bytes 7477248 | tf_op jit(solution)/shard_map/dot_general | solution.py:33
  102.1 1.4 convolution_convert_fusion.2
  103.5 1.4 convolution_convert_fusion.1
  105.0 2.0 shard_map.298
  107.0 2.0 shard_map.299
  109.1 40.4 %shard_map.300 = (f32[256,768]{1,0:T(8,128)S(1)}, bf16[4,256,768]{2,1,0:T(8,128)(2,1)S(1)}, f32[256,768]{1,0:T(8,128)S(1)}, f32[8,768]{1,0:T(8,128)S(1)}, f32[96,768]{1,0:T(8,128)S(1)}, /*index=5*/f32[96,768]{1,0:T(8,128)S(1)}) custom-call(bf16[4,256,768]{2,1,0:T(8,128)(2,1)S(1)} %bitcast.98, bf16[4,256,768]{2,1,0:T(8,128)(2,1)S(1)} %bitcast.99, ...), custom_call_target="tpu_custom_call" | custom-call | flops 20000000000 | bytes 4000000 | tf_op jit(solution)/shard_map/pallas_call | solution.py:780
  150.2 17.0 %shard_map.301 = (bf16[1,1024,576]{2,1,0:T(8,128)(2,1)S(1)}, f32[1,2,192]{2,1,0:T(2,128)S(1)}) custom-call(bf16[1,1024,576]{2,1,0:T(8,128)(2,1)S(1)} %fusion.5.qkv_ref, bf16[1,1024,192]{2,1,0:T(8,128)(2,1)S(1)} %fusion.7.grad_ref, f32[1,3,1024]{2,1,0:T(4,128)S(1)} %bitcast.87), custom_call_target="tpu_custom_call" | custom-call | flops 2013265920 | bytes 6000000 | tf_op jit(solution)/shard_map/pallas_call | solution.py:636
  167.3 2.6 %convolution_convert_fusion = bf16[1024,768]{1,0:T(8,128)(2,1)} fusion(bf16[768,768]{1,0:T(8,128)(2,1)S(1)} %bitcast.86, bf16[1,1024,576]{2,1,0:T(8,128)(2,1)S(1)} %get-tuple-element.64), kind=kOutput, calls=%fused_computation.12 | convolution fusion | flops 906756096 | bytes 3866624 | tf_op jit(solution)/shard_map/dot_general | solution.py:37
  170.2 1.2 shard_map.303
  171.6 1.3 copy-done.3
  172.9 2.0 shard_map.302
  175.2 0.9 copy-done.12
  176.6 27.7 %shard_map.304 = (f32[256,768]{1,0:T(8,128)S(1)}, f32[96,768]{1,0:T(8,128)S(1)}, f32[8,768]{1,0:T(8,128)S(1)}) custom-call(bf16[4,256,768]{2,1,0:T(8,128)(2,1)S(1)} %bitcast.95, f32[256,768]{1,0:T(8,128)S(1)} %bitcast.92, f32[256,768]{1,0:T(8,128)S(1)} %copy-done.21, f32[8,768]{1,0:T(8,128)S(1)} %get-tuple-element.57.vec_ref, ...), custom_call_target="tpu_custom_call" | custom-call | flops 20000000000 | bytes 4000000 | tf_op jit(solution)/shard_map/pallas_call | solution.py:819
  204.9 0.8 fusion.18
  207.4 0.9 copy.64
  208.3 0.9 copy.65
  (89 shorter events, 10.6 us)
Async XLA Ops:
  5.5 1.1 copy-start.8
  6.6 1.1 copy-start.10
  7.8 0.9 copy-start.13
  53.3 1.5 copy-start
  53.3 1.6 copy-start.15
  53.3 2.0 copy-start.18
  53.3 12.9 %copy-start.6 = (bf16[8,96,768]{2,1,0:T(8,128)(2,1)}, bf16[8,96,768]{2,1,0:T(8,128)(2,1)S(1)}, u32[]{:S(2)}) copy-start(bf16[8,96,768]{2,1,0:T(8,128)(2,1)S(1)} %get-tuple-element.56) | copy-start | bytes 3538948
  61.8 2.1 copy-start.24
  66.2 29.2 %copy-start.22 = (bf16[3,64,1024]{2,1,0:T(8,128)(2,1)}, bf16[3,64,1024]{2,1,0:T(8,128)(2,1)S(1)}, u32[]{:S(2)}) copy-start(bf16[3,64,1024]{2,1,0:T(8,128)(2,1)S(1)} %fusion.6) | copy-start | bytes 1179652
  66.2 1.3 copy-start.11
  66.2 1.3 copy-start.14
  67.5 27.9 %copy-start.19 = (bf16[8,96,768]{2,1,0:T(8,128)(2,1)S(1)}, bf16[8,96,768]{2,1,0:T(8,128)(2,1)}, u32[]{:S(2)}) copy-start(bf16[8,96,768]{2,1,0:T(8,128)(2,1)} %copy-done.18) | copy-start | bytes 3538948
  95.4 3.9 %copy-start.16 = (bf16[4,256,768]{2,1,0:T(8,128)(2,1)S(1)}, bf16[4,256,768]{2,1,0:T(8,128)(2,1)}, u32[]{:S(2)}) copy-start(bf16[4,256,768]{2,1,0:T(8,128)(2,1)} %copy-done.15) | copy-start | bytes 4718596
  107.0 2.0 copy-start.9
  109.0 40.4 %copy-start.7 = (bf16[8,96,768]{2,1,0:T(8,128)(2,1)S(1)}, bf16[8,96,768]{2,1,0:T(8,128)(2,1)}, u32[]{:S(2)}) copy-start(bf16[8,96,768]{2,1,0:T(8,128)(2,1)} %copy-done.6) | copy-start | bytes 3538948
  149.5 17.7 %copy-start.4 = (f32[256,768]{1,0:T(8,128)}, f32[256,768]{1,0:T(8,128)S(1)}, u32[]{:S(2)}) copy-start(f32[256,768]{1,0:T(8,128)S(1)} %get-tuple-element.62) | copy-start | bytes 2359300
  149.5 17.7 %copy-start.20 = (f32[256,768]{1,0:T(8,128)}, f32[256,768]{1,0:T(8,128)S(1)}, u32[]{:S(2)}) copy-start(f32[256,768]{1,0:T(8,128)S(1)} %get-tuple-element.65.mixed_grad_ref) | copy-start | bytes 2359300
  167.2 2.6 %copy-start.2 = (bf16[1,1024,576]{2,1,0:T(8,128)(2,1)}, bf16[1,1024,576]{2,1,0:T(8,128)(2,1)S(1)}, u32[]{:S(2)}) copy-start(bf16[1,1024,576]{2,1,0:T(8,128)(2,1)S(1)} %get-tuple-element.64) | copy-start | bytes 3538948
  167.2 2.7 %copy-start.23 = (bf16[3,64,1024]{2,1,0:T(8,128)(2,1)S(1)}, bf16[3,64,1024]{2,1,0:T(8,128)(2,1)}, u32[]{:S(2)}) copy-start(bf16[3,64,1024]{2,1,0:T(8,128)(2,1)} %copy-done.22) | copy-start | bytes 1179652
  170.2 1.4 copy-start.1
  171.6 1.3 copy-start.3
  172.9 2.3 %copy-start.21 = (f32[256,768]{1,0:T(8,128)S(1)}, f32[256,768]{1,0:T(8,128)}, u32[]{:S(2)}) copy-start(f32[256,768]{1,0:T(8,128)} %copy-done.20) | copy-start | bytes 2359300
  174.9 1.1 copy-start.12
  174.9 1.6 copy-start.17
  176.6 30.8 %copy-start.5 = (f32[256,768]{1,0:T(8,128)S(1)}, f32[256,768]{1,0:T(8,128)}, u32[]{:S(2)}) copy-start(f32[256,768]{1,0:T(8,128)} %copy-done.4) | copy-start | bytes 2359300

commit v3 on v2

--- a/solution.py
+++ b/solution.py
@@ -350,6 +350,9 @@
     inner.start()
     low = Gather(low_ref, l_send, l_recv)
     cot = Gather(cot_all_ref, c_send, c_recv)
+    for c in range(cot.chunks):
+        cot_all_ref[t, rows_of(c), :] = cot_ref[rows_of(c), :].astype(BF16)
+        cot.start(c)
     each_peer(dp, lambda k: small_copy(k).wait_recv())
     vec_ref[...] = jnp.sum(small_buf[...], axis=0)
     gain, shift = vec_ref[0:1, :], vec_ref[1:2, :]
@@ -357,9 +360,6 @@
         normed, _ = normed_rows(x_ref[rows_of(c), :])
         low_ref[t, rows_of(c), :] = (normed * gain + shift).astype(BF16)
         low.start(c)
-    for c in range(cot.chunks):
-        cot_all_ref[t, rows_of(c), :] = cot_ref[rows_of(c), :].astype(BF16)
-        cot.start(c)
     pack.forward()
     for c in range(low.chunks):
         low.forward(c)

time: 211 us -> 211 us (level)
  no operation moved by 1% of the time
where the time goes in v3:
time: 211 us
  Pallas kernels  165 us (78%)
  local copies, waits for them, and re-layouts  20.6 us (10%)
  matrix products  19.1 us (9%)
  other arithmetic  4.84 us (2%)
    pallas_call x1, Pallas kernels, on_device(): comm_call(functools.partial(first_kernel, dp), 1, [VM, VM, VM, ANY, ANY],...  44.6 us
    pallas_call x1, Pallas kernels, on_device(): comm_call(functools.partial(third_kernel, dp), 3, [VM] * 7, [((rows, feat...  40.4 us
    pallas_call x1, Pallas kernels, on_device(): comm_call(functools.partial(second_kernel, dp), 2, [VM, VM, VM, ANY], [((...  27.9 us
    pallas_call x1, Pallas kernels, on_device(): comm_call(functools.partial(fourth_kernel, dp), 4, [VM] * 6, [((rows, fea...  27.7 us
    pallas_call x1, Pallas kernels, attend_back(): pl.pallas_call(functools.partial(attend_back_kernel, heads), grid=(clips,...  17 us
    unnamed x55, local copies, waits for them, and re-layouts  11 us
    dot_general x4, matrix products, matmul(): return jnp.dot(left, right, preferred_element_type=F32)  8.79 us
    pallas_call x4, Pallas kernels, token_product(): pl.pallas_call(token_kernel, grid=(m // tile,), out_shape=jax.ShapeDtypeS...  7.26 us

profile of v3, /device:TPU:0, one launch (start us, length us, event | category | flops | bytes accessed | tf_op | source)
XLA Modules:
  0.0 210.6 jit_solution(18053434909557909377)
XLA Ops:
  4.5 1.0 pad_maximum_fusion.1.pack_ref
  5.5 1.1 copy-done.8
  6.6 1.1 copy-done.10
  7.8 0.9 copy-done.13
  8.7 44.6 %shard_map.296 = (bf16[8,96,768]{2,1,0:T(8,128)(2,1)S(1)}, bf16[8,96,768]{2,1,0:T(8,128)(2,1)S(1)}, f32[8,768]{1,0:T(8,128)S(1)}, bf16[4,256,768]{2,1,0:T(8,128)(2,1)S(1)}, bf16[4,256,768]{2,1,0:T(8,128)(2,1)S(1)}) custom-call(f32[256,768]{1,0:T(8,128)S(1)} %bitcast.90, f32[256,768]{1,0:T(8,128)S(1)} %bitcast.88, f32[8,768]{1,0:T(8,128)S(1)} %pad_maximum_fusion.2.small_ref, ...), custom_call_target="tpu_custom_call" | custom-call | flops 20000000000 | bytes 4000000 | tf_op jit(solution)/shard_map/pallas_call | solution.py:721
  53.4 1.4 fusion.5.qkv_ref
  55.3 1.2 fusion.17
  56.6 0.9 copy.45
  57.5 1.2 copy.46
  58.7 1.2 copy.47
  60.0 1.9 multiply_reduce_fusion
  61.8 2.1 exponential_reduce_fusion
  63.9 2.2 %fusion.6 = bf16[3,64,1024]{2,1,0:T(8,128)(2,1)S(1)} fusion(bf16[1024,3,64]{0,2,1:T(8,128)(2,1)S(1)} %bitcast.110, f32[3,1024,1024]{1,2,0:T(8,128)S(1)} %get-tuple-element.93, f32[3,1024]{1,0:T(4,128)S(1)} %log_add_fusion), kind=kOutput, calls=%fused_computation.18 | convolution fusion | flops 412286976 | bytes 13381632 | tf_op jit(solution)/shard_map/while/body/eval_jaxpr/hqk,khd->qhd/dot_general | solution.py:584
  66.2 0.8 convolution_convert_fusion.3
  67.5 27.9 %shard_map.297 = (f32[256,768]{1,0:T(8,128)S(1)}, bf16[4,256,768]{2,1,0:T(8,128)(2,1)S(1)}, bf16[8,96,768]{2,1,0:T(8,128)(2,1)S(1)}) custom-call(bf16[4,256,768]{2,1,0:T(8,128)(2,1)S(1)} %bitcast.76, f32[256,768]{1,0:T(8,128)S(1)} %bitcast.91, f32[8,768]{1,0:T(8,128)S(1)} %get-tuple-element.57.vec_ref, bf16[96,768]{1,0:T(8,128)(2,1)S(1)} %copy-done.14), custom_call_target="tpu_custom_call" | custom-call | flops 20000000000 | bytes 4000000 | tf_op jit(solution)/shard_map/pallas_call | solution.py:753
  95.4 3.9 %multiply_convert_fusion = (bf16[1024,768]{1,0:T(8,128)(2,1)S(1)}, f32[1024,768]{1,0:T(8,128)S(1)}) fusion(f32[768]{0:T(1024)S(1)} %slice_reduce_fusion.1, bf16[1024,768]{1,0:T(8,128)(2,1)S(1)} %bitcast.96, bf16[768,768]{1,0:T(8,128)(2,1)S(1)} %bitcast.100), kind=kOutput, calls=%fused_computation.9 | convolution fusion | flops 1212678144 | bytes 7474176 | tf_op jit(solution)/shard_map/dot_general | solution.py:33
  99.2 2.8 %fusion.16 = (f32[768]{0:T(1024)S(1)}, bf16[1024,768]{1,0:T(8,128)(2,1)S(1)}) fusion(f32[1024,768]{1,0:T(8,128)S(1)} %get-tuple-element.96, f32[768]{0:T(1024)S(1)} %slice_reduce_fusion.1, bf16[1024,768]{1,0:T(8,128)(2,1)S(1)} %bitcast.93, bf16[768,768]{1,0:T(8,128)(2,1)S(1)} %bitcast.102), kind=kOutput, calls=%fused_computation.52 | convolution fusion | flops 1217395968 | bytes 7477248 | tf_op jit(solution)/shard_map/dot_general | solution.py:33
  102.1 1.4 convolution_convert_fusion.2
  103.5 1.4 convolution_convert_fusion.1
  105.0 2.0 shard_map.298
  107.0 2.0 shard_map.299
  109.1 40.4 %shard_map.300 = (f32[256,768]{1,0:T(8,128)S(1)}, bf16[4,256,768]{2,1,0:T(8,128)(2,1)S(1)}, f32[256,768]{1,0:T(8,128)S(1)}, f32[8,768]{1,0:T(8,128)S(1)}, f32[96,768]{1,0:T(8,128)S(1)}, /*index=5*/f32[96,768]{1,0:T(8,128)S(1)}) custom-call(bf16[4,256,768]{2,1,0:T(8,128)(2,1)S(1)} %bitcast.98, bf16[4,256,768]{2,1,0:T(8,128)(2,1)S(1)} %bitcast.99, ...), custom_call_target="tpu_custom_call" | custom-call | flops 20000000000 | bytes 4000000 | tf_op jit(solution)/shard_map/pallas_call | solution.py:780
  150.2 17.0 %shard_map.301 = (bf16[1,1024,576]{2,1,0:T(8,128)(2,1)S(1)}, f32[1,2,192]{2,1,0:T(2,128)S(1)}) custom-call(bf16[1,1024,576]{2,1,0:T(8,128)(2,1)S(1)} %fusion.5.qkv_ref, bf16[1,1024,192]{2,1,0:T(8,128)(2,1)S(1)} %fusion.7.grad_ref, f32[1,3,1024]{2,1,0:T(4,128)S(1)} %bitcast.87), custom_call_target="tpu_custom_call" | custom-call | flops 2013265920 | bytes 6000000 | tf_op jit(solution)/shard_map/pallas_call | solution.py:636
  167.3 2.6 %convolution_convert_fusion = bf16[1024,768]{1,0:T(8,128)(2,1)} fusion(bf16[768,768]{1,0:T(8,128)(2,1)S(1)} %bitcast.86, bf16[1,1024,576]{2,1,0:T(8,128)(2,1)S(1)} %get-tuple-element.64), kind=kOutput, calls=%fused_computation.12 | convolution fusion | flops 906756096 | bytes 3866624 | tf_op jit(solution)/shard_map/dot_general | solution.py:37
  170.2 1.2 shard_map.303
  171.6 1.3 copy-done.3
  172.9 2.0 shard_map.302
  175.2 0.9 copy-done.12
  176.6 27.7 %shard_map.304 = (f32[256,768]{1,0:T(8,128)S(1)}, f32[96,768]{1,0:T(8,128)S(1)}, f32[8,768]{1,0:T(8,128)S(1)}) custom-call(bf16[4,256,768]{2,1,0:T(8,128)(2,1)S(1)} %bitcast.95, f32[256,768]{1,0:T(8,128)S(1)} %bitcast.92, f32[256,768]{1,0:T(8,128)S(1)} %copy-done.21, f32[8,768]{1,0:T(8,128)S(1)} %get-tuple-element.57.vec_ref, ...), custom_call_target="tpu_custom_call" | custom-call | flops 20000000000 | bytes 4000000 | tf_op jit(solution)/shard_map/pallas_call | solution.py:819
  204.9 0.8 fusion.18
  207.4 0.9 copy.64
  208.3 0.9 copy.65
  (89 shorter events, 10.6 us)
Async XLA Ops:
  5.5 1.1 copy-start.8
  6.6 1.1 copy-start.10
  7.8 0.9 copy-start.13
  53.3 1.5 copy-start
  53.3 1.6 copy-start.15
  53.3 2.0 copy-start.18
  53.3 12.9 %copy-start.6 = (bf16[8,96,768]{2,1,0:T(8,128)(2,1)}, bf16[8,96,768]{2,1,0:T(8,128)(2,1)S(1)}, u32[]{:S(2)}) copy-start(bf16[8,96,768]{2,1,0:T(8,128)(2,1)S(1)} %get-tuple-element.56) | copy-start | bytes 3538948
  61.8 2.1 copy-start.24
  66.2 29.2 %copy-start.22 = (bf16[3,64,1024]{2,1,0:T(8,128)(2,1)}, bf16[3,64,1024]{2,1,0:T(8,128)(2,1)S(1)}, u32[]{:S(2)}) copy-start(bf16[3,64,1024]{2,1,0:T(8,128)(2,1)S(1)} %fusion.6) | copy-start | bytes 1179652
  66.2 1.3 copy-start.11
  66.2 1.3 copy-start.14
  67.5 27.9 %copy-start.19 = (bf16[8,96,768]{2,1,0:T(8,128)(2,1)S(1)}, bf16[8,96,768]{2,1,0:T(8,128)(2,1)}, u32[]{:S(2)}) copy-start(bf16[8,96,768]{2,1,0:T(8,128)(2,1)} %copy-done.18) | copy-start | bytes 3538948
  95.4 3.9 %copy-start.16 = (bf16[4,256,768]{2,1,0:T(8,128)(2,1)S(1)}, bf16[4,256,768]{2,1,0:T(8,128)(2,1)}, u32[]{:S(2)}) copy-start(bf16[4,256,768]{2,1,0:T(8,128)(2,1)} %copy-done.15) | copy-start | bytes 4718596
  107.0 2.0 copy-start.9
  109.0 40.4 %copy-start.7 = (bf16[8,96,768]{2,1,0:T(8,128)(2,1)S(1)}, bf16[8,96,768]{2,1,0:T(8,128)(2,1)}, u32[]{:S(2)}) copy-start(bf16[8,96,768]{2,1,0:T(8,128)(2,1)} %copy-done.6) | copy-start | bytes 3538948
  149.5 17.7 %copy-start.4 = (f32[256,768]{1,0:T(8,128)}, f32[256,768]{1,0:T(8,128)S(1)}, u32[]{:S(2)}) copy-start(f32[256,768]{1,0:T(8,128)S(1)} %get-tuple-element.62) | copy-start | bytes 2359300
  149.5 17.7 %copy-start.20 = (f32[256,768]{1,0:T(8,128)}, f32[256,768]{1,0:T(8,128)S(1)}, u32[]{:S(2)}) copy-start(f32[256,768]{1,0:T(8,128)S(1)} %get-tuple-element.65.mixed_grad_ref) | copy-start | bytes 2359300
  167.2 2.6 %copy-start.2 = (bf16[1,1024,576]{2,1,0:T(8,128)(2,1)}, bf16[1,1024,576]{2,1,0:T(8,128)(2,1)S(1)}, u32[]{:S(2)}) copy-start(bf16[1,1024,576]{2,1,0:T(8,128)(2,1)S(1)} %get-tuple-element.64) | copy-start | bytes 3538948
  167.2 2.7 %copy-start.23 = (bf16[3,64,1024]{2,1,0:T(8,128)(2,1)S(1)}, bf16[3,64,1024]{2,1,0:T(8,128)(2,1)}, u32[]{:S(2)}) copy-start(bf16[3,64,1024]{2,1,0:T(8,128)(2,1)} %copy-done.22) | copy-start | bytes 1179652
  170.2 1.4 copy-start.1
  171.6 1.3 copy-start.3
  172.9 2.3 %copy-start.21 = (f32[256,768]{1,0:T(8,128)S(1)}, f32[256,768]{1,0:T(8,128)}, u32[]{:S(2)}) copy-start(f32[256,768]{1,0:T(8,128)} %copy-done.20) | copy-start | bytes 2359300
  174.9 1.1 copy-start.12
  174.9 1.6 copy-start.17
  176.6 30.8 %copy-start.5 = (f32[256,768]{1,0:T(8,128)S(1)}, f32[256,768]{1,0:T(8,128)}, u32[]{:S(2)}) copy-start(f32[256,768]{1,0:T(8,128)} %copy-done.4) | copy-start | bytes 2359300
